TPU v7x, 32 devices: a whole 2x2x4 slice. The times are simulated.
32 devices in a mesh: prow: 4 (over y, x), pcol: 8 (over z, core).
Axes of the slice: x: 2, y: 2, z: 4, core: 2. Of those that a mesh axis runs over, the one named last changes fastest.
Arguments:
- ainv: float32 [16384, 16384], P('prow', 'pcol'), as said below
- panels: float32 [3, 16384, 512], P(None, 'prow', 'pcol'), may hold values from -0.53 to 0.53
- pattern: int32 [3, 128], replicated, may hold values 0 or 1
- coupling: float32 [3, 512, 512], replicated, may hold values from -0.25 to 0.25
- dinv: float32 [3, 512, 512], replicated, as said below
Outputs:
- xpanel: float32 [3, 16384, 512], P(None, 'prow', 'pcol')
- xcross: float32 [3, 512, 512], P(None, 'pcol')
- ydiag: float32 [3, 512, 512], P(None, 'pcol')
Inputs may be any that keep to these rules, and one draw needn't show every extreme that they name: ainv is symmetric: ainv equals its transpose up to rounding. Each dinv[k] is symmetric: it equals its transpose exactly.
All inputs are finite; a program needn't handle non-finite values.
Results may differ from a plain program's by a relative error of at most 0.000092.
Values sent between devices are 32-bit elements; how exact they have to be, the bound alone decides.
No kernel may reach another device: no remote copies, remote signals or barrier semaphores. Data moves between devices by JAX's collectives and lax.ppermute only.
A program may use at most 192 MiB of HBM per device.

v0:
```python
import jax
import jax.numpy as jnp
from jax import lax
from jax.sharding import PartitionSpec as P

NB = 128


precise = lax.Precision.HIGHEST


def broadcast(shard, axis, root):
    mine = lax.axis_index(axis) == root
    return lax.psum(jnp.where(mine, shard, jnp.zeros_like(shard)), axis)


def matmul(left, right):
    return jnp.dot(left, right, precision=precise, preferred_element_type=jnp.float32)


def tdot(left, right):
    return lax.dot_general(
        left, right, (((0,), (0,)), ((), ())), precision=precise, preferred_element_type=jnp.float32
    )


def stacked_inner(columns, factor):
    return lax.dot_general(
        columns,
        factor,
        (((1,), (0,)), ((), ())),
        precision=precise,
        preferred_element_type=jnp.float32,
    )


def shards(ainv, panels, pattern, coupling, dinv):
    row_count = lax.axis_size("prow")
    col_count = lax.axis_size("pcol")
    row_index = lax.axis_index("prow")
    col_index = lax.axis_index("pcol")
    local_rows = panels.shape[1]
    local_cols = panels.shape[2]
    cross_rows = ainv.shape[1]
    blocks_here = local_rows // NB
    flags = lax.dynamic_slice_in_dim(pattern, row_index * blocks_here, blocks_here, 1)
    row_mask = jnp.repeat(flags.astype(jnp.float32), NB, axis=1)
    masked = panels * row_mask[:, :, None]
    row_panels = lax.all_gather(masked, "pcol", axis=2, tiled=True)
    ratio = col_count // row_count
    offset = col_index % ratio * cross_rows
    root = col_index // ratio
    first, second, third = (coupling[0], coupling[1], coupling[2])
    my_start = col_index * local_cols

    def own_rows(matrix):
        return lax.dynamic_slice_in_dim(matrix, my_start, local_cols, 0)

    finished = []
    inner = []
    for section in range(3):
        sent = lax.dynamic_slice_in_dim(row_panels[section], offset, cross_rows, 0)
        crossed = broadcast(sent, "prow", root)
        partial_value = matmul(ainv, crossed)
        if section == 1:
            partial_value = partial_value + matmul(finished[0], own_rows(first))
        if section == 2:
            partial_value = (
                partial_value
                + matmul(finished[0], own_rows(second))
                + matmul(finished[1], own_rows(third))
            )
        current = -lax.psum_scatter(partial_value, "pcol", scatter_dimension=1, tiled=True)
        finished.append(current)
        terms = stacked_inner(jnp.stack(finished, 0), row_panels[section])
        summed = lax.psum(terms, "prow")
        inner.append(lax.all_gather(summed, "pcol", axis=1, tiled=True))
    result = jnp.stack(finished, 0)
    diag_zero = dinv[0] - inner[0][0].T
    cross_one = -(inner[1][0] + matmul(diag_zero, first))
    diag_one = dinv[1] - inner[1][1].T - tdot(first, cross_one)
    cross_two = -(inner[2][0] + matmul(diag_zero, second) + matmul(cross_one, third))
    cross_three = -(inner[2][1] + tdot(cross_one, second) + matmul(diag_one, third))
    diag_two = dinv[2] - inner[2][2].T - tdot(second, cross_two) - tdot(third, cross_three)
    xcross = lax.dynamic_slice_in_dim(
        jnp.stack([cross_one, cross_two, cross_three], 0), my_start, local_cols, 1
    )
    ydiag = lax.dynamic_slice_in_dim(
        jnp.stack([diag_zero, diag_one, diag_two], 0), my_start, local_cols, 1
    )
    return (result, xcross, ydiag)


def solution(mesh):
    placed = (P("prow", "pcol"), P(None, "prow", "pcol"), P(), P(), P())
    return jax.shard_map(
        shards,
        mesh=mesh,
        in_specs=placed,
        out_specs=(P(None, "prow", "pcol"), P(None, "pcol", None), P(None, "pcol", None)),
        check_vma=False,
    )
```

profile of v0, /device:TPU:0, one launch (start us, length us, event | category | flops | bytes accessed | tf_op | source)
XLA Modules:
  0.0 1181.2 jit_solution(15338208754666558292)
XLA Ops:
  7.2 0.8 fusion.48
  8.0 0.1 broadcast_bitcast_fusion
  8.1 4.0 broadcast_multiply_fusion
  12.1 0.0 all-reduce.7.cloned.1.call-start
  12.2 222.6 %all-gather.5.cloned.1.call-done = f32[3,4096,512]{1,2,0:T(8,128)} async-done(((f32[3,4096,64]{1,2,0:T(8,128)}), f32[3,4096,512]{1,2,0:T(8,128)}) %all-gather.5.cloned.1.call-update) | async-done | bytes 25165840 | tf_op jit(solution)/shard_map/all_gather | solution.py:49
  234.8 17.5 %fusion.62 = (f32[1,4096,512]{1,2,0:T(8,128)}, f32[1,4096,512]{1,2,0:T(8,128)}, f32[1,4096,512]{1,2,0:T(8,128)}) fusion(f32[3,4096,512]{1,2,0:T(8,128)} %all-gather.5.cloned.1.call-done), kind=kLoop, calls=%fused_computation.97 | loop fusion | bytes 50331648 | tf_op jit(solution)/shard_map/slice | solution.py:62
  252.3 4.7 constant_dynamic-slice_fusion.2
  257.1 5.4 copy.35
  262.4 7.8 constant_dynamic-slice_fusion
  270.2 5.4 copy.37
  275.6 4.9 select_bitcast_fusion.2
  280.5 2.5 select_bitcast_fusion
  283.0 5.4 copy.36
  288.4 4.7 select_bitcast_fusion.1
  293.1 0.0 reduce-scatter.4.cloned.1.call-start
  293.1 239.1 %all-reduce.7.cloned.1.call-done = (f32[2048,512]{1,0:T(8,128)}, f32[2048,512]{1,0:T(8,128)}, f32[2048,512]{1,0:T(8,128)}) async-done(((f32[2048,512]{1,0:T(8,128)}, f32[2048,512]{1,0:T(8,128)}, f32[2048,512]{1,0:T(8,128)}), (f32[2048,512]{1,0:T(8,128)}, f32[2048,512]{1,0:T(8,128)}, f32[2048,512]{1,0:T(8,128)})) %all-reduce.7.cloned.1.call-update) | async-done | bytes 12582928 | tf_op jit(solution)/shard_map/psum | solution.py:14
  532.3 111.5 %convolution_bitcast_fusion = f32[4096,512]{0,1:T(8,128)} fusion(f32[2048,512]{1,0:T(8,128)} %get-tuple-element.12, f32[4096,2048]{1,0:T(8,128)} %param.5), kind=kOutput, calls=%fused_computation.9 | convolution fusion | flops 51539607552 | bytes 46137344 | tf_op jit(solution)/shard_map/dot_general | solution.py:18
  643.8 0.0 reduce-scatter.6.cloned.1.call-start
  643.8 1.8 copy-done
  645.6 1.7 fusion.64
  647.4 1.6 copy-done.21
  648.9 111.8 %fusion.65 = f32[512,4096]{1,0:T(8,128)} fusion(f32[2048,512]{1,0:T(8,128)S(1)} %copy-done.21, f32[4096,2048]{1,0:T(8,128)} %param.5), kind=kOutput, calls=%fused_computation.100 | convolution fusion | flops 51539607552 | bytes 46137344 | tf_op jit(solution)/shard_map/dot_general | solution.py:18
  760.8 11.6 bitcast_add_fusion.1
  772.4 0.0 reduce-scatter.8.cloned.1.call-start
  772.4 111.7 %fusion.66 = f32[512,4096]{1,0:T(8,128)} fusion(f32[2048,512]{1,0:T(8,128)} %get-tuple-element.13, f32[4096,2048]{1,0:T(8,128)} %param.5), kind=kOutput, calls=%fused_computation.101 | convolution fusion | flops 51539607552 | bytes 46137344 | tf_op jit(solution)/shard_map/dot_general | solution.py:18
  884.2 9.8 fusion.32
  894.0 14.5 %fusion.6 = f32[4096,512]{0,1:T(8,128)} fusion(f32[4096,512]{0,1:T(8,128)} %fusion.32, f32[512,4096]{1,0:T(8,128)} %fusion.66, f32[4096,64]{0,1:T(8,128)} %reduce-scatter.6.cloned.1.call-done, f32[1,512,512]{2,1,0:T(8,128)} %get-tuple-element.21, s32[]{:T(128)S(6)} %select_n.60), kind=kOutput, calls=%fused_computation.7 | convolution fusion | flops 1615069184 | bytes 26345476 | tf_op jit(solution)/shard_map/dot_general | solution.py:18
  908.6 0.0 all-reduce.5.cloned.1.call-start
  908.6 12.5 %fusion.17 = f32[1,64,512]{2,1,0:T(8,128)} fusion(f32[4096,64]{0,1:T(8,128)} %reduce-scatter.4.cloned.1.call-done, f32[3,4096,512]{1,2,0:T(8,128)} %all-gather.5.cloned.1.call-done), kind=kOutput, calls=%fused_computation.39 | convolution fusion | flops 1610874880 | bytes 9568256 | tf_op jit(solution)/shard_map/dot_general | solution.py:28
  921.1 0.1 negate_bitcast_fusion.2
  921.3 0.1 negate_bitcast_fusion.1
  921.3 0.9 copy-done.13
  922.2 1.0 copy-done.14
  923.2 13.0 %fusion.4 = f32[2,64,512]{2,1,0:T(8,128)} fusion(f32[1,4096,64]{1,2,0:T(8,128)S(1)} %negate_bitcast_fusion.1, f32[1,4096,64]{1,2,0:T(8,128)S(1)} %negate_bitcast_fusion.2, f32[3,4096,512]{1,2,0:T(8,128)} %all-gather.5.cloned.1.call-done), kind=kOutput, calls=%fused_computation.4 | convolution fusion | flops 3221749760 | bytes 10747904 | tf_op jit(solution)/shard_map/dot_general | solution.py:28
  936.2 62.4 %reduce-scatter.8.cloned.1.call-done = f32[4096,64]{0,1:T(8,128)} async-done(((f32[4096,512]{0,1:T(8,128)}), f32[4096,64]{0,1:T(8,128)}) %reduce-scatter.8.cloned.1.call-update) | async-done | bytes 1048592 | tf_op jit(solution)/shard_map/reduce_scatter | solution.py:73
  998.6 1.3 negate_bitcast_fusion
  1000.0 1.8 pad_maximum_fusion
  1001.8 1.7 copy-done.7
  1003.4 11.5 fusion
  1015.0 0.0 all-gather.9.cloned.1.call-start
  1015.0 47.7 %all-reduce.5.cloned.1.call-done = (f32[2,64,512]{2,1,0:T(8,128)}, f32[1,64,512]{2,1,0:T(8,128)}, f32[3,64,512]{2,1,0:T(8,128)}) async-done(((f32[2,64,512]{2,1,0:T(8,128)}, f32[1,64,512]{2,1,0:T(8,128)}, f32[3,64,512]{2,1,0:T(8,128)}), (f32[2,64,512]{2,1,0:T(8,128)}, f32[1,64,512]{2,1,0:T(8,128)}, f32[3,64,512]{2,1,0:T(8,128)})) %all-reduce.5.cloned.1.call-update) | async-done | bytes 786448 | tf_op jit(solution)/shard_map/psum | solution.py:76
  1062.8 0.7 all-gather.7.cloned.1.call-update
  1063.5 0.0 all-gather.11.cloned.1.call-start
  1063.5 0.7 all-gather.11.cloned.1.call-update
  1064.2 3.7 fusion.63
  1067.9 2.5 copy.32
  1070.4 2.6 copy.33
  1073.0 2.5 copy.34
  1075.5 11.0 all-gather.9.cloned.1.call-done
  1086.5 2.7 fusion.50
  1089.2 27.7 %all-gather.7.cloned.1.call-done = f32[2,512,512]{2,1,0:T(8,128)} async-done(((f32[2,64,512]{2,1,0:T(8,128)}), f32[2,512,512]{2,1,0:T(8,128)}) %all-gather.7.cloned.1.call-update) | async-done | bytes 2097168 | tf_op jit(solution)/shard_map/all_gather | solution.py:77
  1117.0 4.0 fusion.16
  1121.0 1.1 copy-done.1
  1122.0 3.0 fusion.14
  1125.0 31.5 %all-gather.11.cloned.1.call-done = f32[3,512,512]{2,1,0:T(8,128)} async-done(((f32[3,64,512]{2,1,0:T(8,128)}), f32[3,512,512]{2,1,0:T(8,128)}) %all-gather.11.cloned.1.call-update) | async-done | bytes 3145744 | tf_op jit(solution)/shard_map/all_gather | solution.py:77
  1156.5 3.9 convolution_add_fusion.3
  1160.4 1.9 fusion.15
  1162.3 1.9 convolution_add_fusion.1
  1164.3 2.1 fusion.13
  1166.5 1.9 fusion.12
  1168.4 1.9 fusion.11
  1170.4 1.2 fusion.36
  1171.5 2.2 copy.25
  1173.7 0.8 fusion.38
  (50 shorter events, 0.3 us)
Async XLA Ops:
  7.2 227.6 %all-gather.5.cloned.1.call-start = ((), (), s32[]{:S(2)}) async-start(), calls=%async_computation.3 | async-start | bytes 28311552 | tf_op jit(solution)/shard_map/all_gather | solution.py:49
  12.1 520.2 %all-reduce.7.cloned.1.call-start = ((), (), s32[]{:S(2)}) async-start(), calls=%async_computation.11 | async-start | bytes 25165824 | tf_op jit(solution)/shard_map/psum | solution.py:14
  275.6 4.9 copy-start.6
  293.1 467.7 %reduce-scatter.4.cloned.1.call-start = ((), (), s32[]{:S(2)}) async-start(), calls=%async_computation.4 | async-start | bytes 9437184 | tf_op jit(solution)/shard_map/reduce_scatter | solution.py:73
  643.7 1.9 copy-start
  643.8 250.3 %reduce-scatter.6.cloned.1.call-start = ((), (), s32[]{:S(2)}) async-start(), calls=%async_computation.5 | async-start | bytes 9437184 | tf_op jit(solution)/shard_map/reduce_scatter | solution.py:73
  645.6 3.3 copy-start.21
  772.4 226.3 %reduce-scatter.8.cloned.1.call-start = ((), (), s32[]{:S(2)}) async-start(), calls=%async_computation.6 | async-start | bytes 9437184 | tf_op jit(solution)/shard_map/reduce_scatter | solution.py:73
  772.4 111.8 %copy-start.4 = (f32[4096,64]{0,1:T(8,128)S(1)}, f32[4096,64]{0,1:T(8,128)}, u32[]{:S(2)}) copy-start(f32[4096,64]{0,1:T(8,128)} %reduce-scatter.4.cloned.1.call-done) | copy-start | bytes 3145732
  908.6 154.1 %all-reduce.5.cloned.1.call-start = ((), (), s32[]{:S(2)}) async-start(), calls=%async_computation.10 | async-start | bytes 1572864 | tf_op jit(solution)/shard_map/psum | solution.py:76
  908.6 12.5 %copy-start.5 = (f32[4096,64]{0,1:T(8,128)S(1)}, f32[4096,64]{0,1:T(8,128)}, u32[]{:S(2)}) copy-start(f32[4096,64]{0,1:T(8,128)} %reduce-scatter.4.cloned.1.call-done) | copy-start | bytes 3145732
  908.6 12.6 %copy-start.15 = (f32[4096,64]{0,1:T(8,128)S(1)}, f32[4096,64]{0,1:T(8,128)}, u32[]{:S(2)}) copy-start(f32[4096,64]{0,1:T(8,128)} %reduce-scatter.6.cloned.1.call-done) | copy-start | bytes 3145732
  921.2 1.0 copy-start.13
  922.2 1.0 copy-start.14
  1001.7 1.7 copy-start.7
  1015.0 71.5 %all-gather.9.cloned.1.call-start = ((), (), s32[]{:S(2)}) async-start(), calls=%async_computation.8 | async-start | bytes 1179648 | tf_op jit(solution)/shard_map/all_gather | solution.py:77
  1062.7 54.2 %all-gather.7.cloned.1.call-start = ((), (), s32[]{:S(2)}) async-start(), calls=%async_computation.7 | async-start | bytes 2359296 | tf_op jit(solution)/shard_map/all_gather | solution.py:77
  1063.5 93.0 %all-gather.11.cloned.1.call-start = ((), (), s32[]{:S(2)}) async-start(), calls=%async_computation.9 | async-start | bytes 3538944 | tf_op jit(solution)/shard_map/all_gather | solution.py:77
  1117.0 5.1 copy-start.17
  1117.0 5.1 copy-start.20
  1120.9 1.1 copy-start.1
  1156.5 3.9 copy-start.2
  1156.5 5.8 copy-start.19
  1160.4 3.9 copy-start.8
  1162.3 4.1 copy-start.9
  1162.3 4.1 copy-start.16
  1166.4 3.9 copy-start.11
  1166.5 3.9 copy-start.18
  1170.3 3.4 copy-start.3
  1170.3 3.4 copy-start.10
  1170.4 3.3 copy-start.12
Sparse Core Ops, SparseCore 0:
  12.2 222.5 all-gather.4
  293.2 239.0 all-reduce.6
  643.9 89.5 reduce-scatter.3
  772.5 89.9 reduce-scatter.5
  908.7 89.9 reduce-scatter.7
  1015.1 47.5 all-reduce.4
  1064.4 22.0 all-gather.8
  1088.2 28.7 all-gather.6
  1118.7 37.7 all-gather.10
where the time goes:
time: 1190 us; the launch traced here: 1180 us
  waiting for transfers between devices  644 us (54%)
  matrix products  429 us (36%)
  local copies, waits for them, and re-layouts  69.6 us (6%)
  other arithmetic  24.7 us (2%)
  between operations  14.4 us (1%)
    dot_general x10, matrix products, matmul(): jnp.dot(left, right, precision=precise, preferred_element_type=jnp.float32)  383 us
    psum x1, waiting for transfers between devices, broadcast(): return lax.psum(jnp.where(mine, shard, jnp.zeros_like(shard)), axis)  239 us
    all_gather x1, waiting for transfers between devices, shards(): row_panels = lax.all_gather(masked, 'pcol', axis=2, tiled=True)  223 us
    all_gather x3, waiting for transfers between devices, shards(): inner.append(lax.all_gather(summed, 'pcol', axis=1, tiled=True))  70.2 us
    reduce_scatter x3, waiting for transfers between devices, shards(): lax.psum_scatter(partial_value, 'pcol', scatter_dimension=1, tiled=True)  62.5 us
    psum x1, waiting for transfers between devices, shards(): summed = lax.psum(terms, 'prow')  47.7 us
    dot_general x3, matrix products, stacked_inner(): lax.dot_general(columns, factor, (((1,), (0,)), ((), ())), precision=prec...  37 us
    unnamed x53, local copies, waits for them, and re-layouts  34.1 us
  transfers between devices with their start and end apart: 9, of which 7 were waited for; matrix products, arithmetic and copies ran while one was open for 24% of the time, Pallas kernels for 0%

commit v1 on v0

v1 whole, which is shorter than its diff:
```python
import jax
import jax.numpy as jnp
from jax import lax
from jax.sharding import PartitionSpec as P

NB = 128

precise = lax.Precision.HIGHEST


def matmul(left, right):
    return jnp.dot(left, right, precision=precise, preferred_element_type=jnp.float32)


def tdot(left, right, precision=precise):
    return lax.dot_general(
        left, right, (((0,), (0,)), ((), ())), precision=precision, preferred_element_type=jnp.float32
    )


def split(values):
    high = lax.reduce_precision(values, exponent_bits=8, mantissa_bits=7)
    return high.astype(jnp.bfloat16), (values - high).astype(jnp.bfloat16)


def exchange(value, axis, size, step):
    return lax.ppermute(value, axis, [(i, i ^ step) for i in range(size)])


def shards(ainv, panels, pattern, coupling, dinv):
    rows_n = lax.axis_size("prow")
    cols_n = lax.axis_size("pcol")
    row = lax.axis_index("prow")
    col = lax.axis_index("pcol")
    local_rows, local_cols = panels.shape[1:]
    width = ainv.shape[1]
    part = width // rows_n
    ratio = cols_n // rows_n
    half = local_cols // 2
    blocks_here = local_rows // NB

    flags = lax.dynamic_slice_in_dim(pattern, row * blocks_here, blocks_here, 1)
    mask = jnp.repeat(flags.astype(jnp.float32), NB, axis=1)
    shard = jnp.swapaxes(panels, 1, 2) * mask[:, None, :]

    chunks = [(0, 0, local_cols), (1, 0, local_cols), (2, 0, half), (2, half, local_cols)]
    gathered = [
        lax.all_gather(shard[j, lo:hi], "pcol", axis=0, tiled=True) for j, lo, hi in chunks
    ]

    inverse = []
    for step in range(rows_n):
        piece = lax.dynamic_slice_in_dim(ainv, (row ^ step) * part, part, 1)
        high, low = split(piece)
        inverse.append(jnp.concatenate([high, low, high], 0))

    def columns(matrix, lo, hi):
        whole = matrix.shape[0]
        return matrix.reshape(whole, cols_n, local_cols)[:, :, lo:hi].reshape(whole, -1)

    def triple(values):
        high, low = split(values)
        return jnp.concatenate([high, high, low], 1)

    high_precision = lax.Precision.HIGH
    eliminated = []
    for (j, lo, hi), value in zip(chunks, gathered):
        if j == 1:
            value = value - tdot(coupling[0], eliminated[0], high_precision)
        if j == 2:
            value = value - (
                tdot(columns(coupling[1], lo, hi), eliminated[0], high_precision)
                + tdot(columns(coupling[2], lo, hi), eliminated[1], high_precision)
            )
        eliminated.append(value)
    factors = [triple(value) for value in eliminated]

    finished = []
    for value in factors:
        products = [
            jnp.dot(value, inverse[step], preferred_element_type=jnp.float32)
            for step in range(rows_n)
        ]
        total = products[0]
        for step in range(1, rows_n):
            total = total + exchange(products[step], "prow", rows_n, step)
        count = total.shape[0] // cols_n
        moved = lax.all_to_all((-total).reshape(cols_n, count, part), "pcol", 0, 0)
        moved = lax.all_to_all(moved.reshape(rows_n, ratio, count, part), "prow", 0, 0)
        finished.append(moved.transpose(2, 1, 0, 3).reshape(count, local_rows))

    inner = [[], [], []]
    for (j, lo, hi), value in zip(chunks, finished):
        high, low = split(-value)
        left = jnp.concatenate([high, low, high], 1)
        terms = []
        for (k, first, last), right in zip(chunks, factors):
            if k < j:
                continue
            term = lax.dot_general(
                left, right, (((1,), (1,)), ((), ())), preferred_element_type=jnp.float32
            )
            terms.append(term)
        term = jnp.concatenate(terms, 1)
        summed = term
        for step in range(1, rows_n):
            summed = summed + exchange(term, "prow", rows_n, step)
        blocks = []
        for k in range(j, 3):
            pieces = []
            for k2, first, last in chunks:
                if k2 == k:
                    size = cols_n * (last - first)
                    pieces.append(summed[:, :size].reshape(hi - lo, cols_n, last - first))
                    summed = summed[:, size:]
            blocks.append(jnp.concatenate(pieces, 2).reshape(hi - lo, cols_n * local_cols))
        inner[j].append(blocks)
    inner = [[jnp.concatenate(b, 0) for b in zip(*parts)] for parts in inner]

    first, second, third = coupling[0], coupling[1], coupling[2]
    start = col * local_cols

    def own_rows(matrix):
        return lax.dynamic_slice_in_dim(matrix, start, local_cols, 0)

    def own_cols(matrix):
        return lax.dynamic_slice_in_dim(matrix, start, local_cols, 1)

    bridge = second - matmul(first, third)
    d0 = own_rows(dinv[0])
    d1 = own_rows(dinv[1])
    k0 = tdot(own_cols(first), dinv[0])
    k1 = tdot(own_cols(bridge), dinv[0])
    k2 = tdot(own_cols(third), dinv[1])
    diag_zero = d0 + inner[0][0]
    cross_one = inner[0][1] - matmul(d0, first)
    cross_two = inner[0][2] - matmul(d0, bridge)
    diag_one = inner[1][0] + (d1 + matmul(k0, first))
    cross_three = inner[1][1] + (matmul(k0, bridge) - matmul(d1, third))
    diag_two = inner[2][0] + (own_rows(dinv[2]) + matmul(k1, bridge) + matmul(k2, third))

    panel_parts = [[], [], []]
    for (j, lo, hi), value in zip(chunks, finished):
        panel_parts[j].append(value)
    xpanel = jnp.stack([jnp.concatenate(p, 0) for p in panel_parts], 0)
    xcross = jnp.stack([cross_one, cross_two, cross_three], 0)
    ydiag = jnp.stack([diag_zero, diag_one, diag_two], 0)
    return (jnp.swapaxes(xpanel, 1, 2), xcross, ydiag)


def solution(mesh):
    placed = (P("prow", "pcol"), P(None, "prow", "pcol"), P(), P(), P())
    return jax.shard_map(
        shards,
        mesh=mesh,
        in_specs=placed,
        out_specs=(P(None, "prow", "pcol"), P(None, "pcol", None), P(None, "pcol", None)),
        check_vma=False,
    )
```

time: 1190 us -> 931 us (0.78)
  waiting for transfers between devices: 644 us -> 267 us
  starting transfers between devices: 0.37 us -> 61.2 us
  other arithmetic: 24.7 us -> 67.4 us
  local copies, waits for them, and re-layouts: 69.6 us -> 108 us
  matrix products: 429 us -> 404 us
    dot_general x10 -> x8, matrix products: 383 us -> 17.9 us  [matmul(): jnp.dot(left, right, precision=precise, preferred_element_type=jnp.float32)]
    dot_general x7 -> x35, matrix products: 45.8 us -> 386 us  [the longest x16 268 us: shards(): jnp.dot(value, inverse[step], preferred_element_type=jnp.float32)]
    psum x2 -> x0, waiting for transfers between devices: 287 us -> none  [the longest x1 239 us: broadcast(): return lax.psum(jnp.where(mine, shard, jnp.zeros_like(shard)), axis)]
    all_gather x4, waiting for transfers between devices: 293 us -> 168 us  [shards(): lax.all_gather(shard[j, lo:hi], 'pcol', axis=0, tiled=True)]
    ppermute x0 -> x24, waiting for transfers between devices: none -> 64.2 us  [exchange(): return lax.ppermute(value, axis, [(i, i ^ step) for i in range(size)])]
    reduce_scatter x3 -> x0, waiting for transfers between devices: 62.5 us -> none  [shards(): lax.psum_scatter(partial_value, 'pcol', scatter_dimension=1, tiled=True)]
    convert_element_type x1 -> x7, other arithmetic: 0.76 us -> 41.3 us  [the longest x6 40.5 us: split(): return (high.astype(jnp.bfloat16), (values - high).astype(jnp.bfloat16))]
    all_gather x0 -> x3, local copies, waits for them, and re-layouts: none -> 39.9 us  [shards(): lax.all_gather(shard[j, lo:hi], 'pcol', axis=0, tiled=True)]
  transfers between devices with their start and end apart: 9 -> 36, of which waited for: 7 -> 12; matrix products, arithmetic and copies ran while one was open for 24% -> 30% of each run, Pallas kernels for 0% -> 0%
where the time goes in v1:
time: 931 us; the launch traced here: 923 us
  matrix products  404 us (43%)
  waiting for transfers between devices  267 us (29%)
  local copies, waits for them, and re-layouts  108 us (12%)
  other arithmetic  67.4 us (7%)
  starting transfers between devices  61.2 us (7%)
  between operations  15.1 us (2%)
    dot_general x16, matrix products, shards(): jnp.dot(value, inverse[step], preferred_element_type=jnp.float32)  268 us
    all_gather x4, waiting for transfers between devices, shards(): lax.all_gather(shard[j, lo:hi], 'pcol', axis=0, tiled=True)  168 us
    dot_general x8, matrix products, tdot(): lax.dot_general(left, right, (((0,), (0,)), ((), ())), precision=precisio...  84.2 us
    ppermute x24, waiting for transfers between devices, exchange(): return lax.ppermute(value, axis, [(i, i ^ step) for i in range(size)])  64.2 us
    convert_element_type x6, other arithmetic, split(): return (high.astype(jnp.bfloat16), (values - high).astype(jnp.bfloat16))  40.5 us
    all_gather x3, local copies, waits for them, and re-layouts, shards(): lax.all_gather(shard[j, lo:hi], 'pcol', axis=0, tiled=True)  39.9 us
    dot_general x11, matrix products, shards(): lax.dot_general(left, right, (((1,), (1,)), ((), ())), preferred_element_...  33.6 us
    ppermute x24, starting transfers between devices, exchange(): return lax.ppermute(value, axis, [(i, i ^ step) for i in range(size)])  29.5 us
  transfers between devices with their start and end apart: 36, of which 12 were waited for; matrix products, arithmetic and copies ran while one was open for 30% of the time, Pallas kernels for 0%

profile of v1, /device:TPU:0, one launch (start us, length us, event | category | flops | bytes accessed | tf_op | source)
XLA Modules:
  0.0 923.3 jit_solution(17177254837875699897)
XLA Ops:
  8.1 4.1 fusion.37
  17.1 7.0 fusion.143
  26.6 2.6 copy.88
  29.1 2.6 copy.89
  33.9 3.2 convolution_subtract_fusion
  46.7 24.7 %fusion.1 = (bf16[4096,512]{1,0:T(8,128)(2,1)}, bf16[4096,512]{1,0:T(8,128)(2,1)}, bf16[4096,512]{1,0:T(8,128)(2,1)}, bf16[4096,512]{1,0:T(8,128)(2,1)}, bf16[40...) fusion(f32[4096,2048]{1,0:T(8,128)} %param.5, ...), kind=kLoop, calls=%fused_computation.19 | loop fusion | flops 33554432 | bytes 67108880 | tf_op jit(solution)/shard_map/convert_element_type | solution.py:23
  71.4 10.3 %copy.69 = f32[1,256,4096]{1,2,0:T(8,128)} copy(f32[1,256,4096]{2,0,1:T(1,128)} %all-gather.13.cloned.1.call-done) | data formatting | bytes 8388608 | tf_op jit(solution)/shard_map/all_gather | solution.py:48
  81.8 32.0 %all-gather.15.cloned.1.call-done = f32[1,256,4096]{2,0,1:T(1,128)} async-done(((f32[1,32,4096]{2,0,1:T(1,128)}), f32[1,256,4096]{2,0,1:T(1,128)}) %all-gather.15.cloned.1.call-update) | async-done | bytes 4194320 | tf_op jit(solution)/shard_map/all_gather | solution.py:48
  113.8 10.3 %copy.74 = f32[1,256,4096]{1,2,0:T(8,128)} copy(f32[1,256,4096]{2,0,1:T(1,128)} %all-gather.15.cloned.1.call-done) | data formatting | bytes 8388608 | tf_op jit(solution)/shard_map/all_gather | solution.py:48
  124.1 72.1 %all-gather.11.cloned.1.call-done = f32[1,512,4096]{2,0,1:T(1,128)} async-done(((f32[1,64,4096]{2,0,1:T(1,128)}), f32[1,512,4096]{2,0,1:T(1,128)}) %all-gather.11.cloned.1.call-update) | async-done | bytes 8388624 | tf_op jit(solution)/shard_map/all_gather | solution.py:48
  196.2 19.2 %copy.65 = f32[1,512,4096]{1,2,0:T(8,128)} copy(f32[1,512,4096]{2,0,1:T(1,128)} %all-gather.11.cloned.1.call-done) | data formatting | bytes 16777216 | tf_op jit(solution)/shard_map/all_gather | solution.py:48
  215.5 63.4 %all-gather.9.cloned.1.call-done = f32[1,512,4096]{2,0,1:T(1,128)} async-done(((f32[1,64,4096]{2,0,1:T(1,128)}), f32[1,512,4096]{2,0,1:T(1,128)}) %all-gather.9.cloned.1.call-update) | async-done | bytes 8388624 | tf_op jit(solution)/shard_map/all_gather | solution.py:48
  278.9 37.5 %reduce-precision_convert_fusion = (bf16[512,4096]{0,1:T(8,128)(2,1)}, bf16[512,4096]{0,1:T(8,128)(2,1)}, f32[512,4096]{0,1:T(8,128)S(1)}) fusion(f32[3,512,512]{2,1,0:T(8,128)S(1)} %copy-done, f32[1,512,4096]{2,0,1:T(1,128)} %all-gather.9.cloned.1.call-done, f32[1,512,4096]{1,2,0:T(8,128)} %copy.65), kind=kOutput, calls=%fused_computation.7 | convolution fusion | flops 6452936704 | bytes 34603008 | tf_op jit(solution)/shard_map/dot_general | solution.py:16
  316.4 5.0 fusion.153
  321.5 3.7 fusion.152
  325.2 15.2 %reduce-precision_convert_fusion.7 = (bf16[256,4096]{0,1:T(8,128)(2,1)S(1)}, bf16[256,4096]{0,1:T(8,128)(2,1)}) fusion(f32[4096,256]{1,0:T(8,128)S(1)} %fusion.152, f32[512,256]{0,1:T(8,128)S(1)} %bitcast.182, f32[1,512,4096]{2,0,1:T(1,128)} %all-gather.9.cloned.1.call-done, f32[1,256,4096]{1,2,0:T(8,128)S(1)} %copy-done.3), kind=kOutput, calls=%fused_computation.39 | convolution fusion | flops 3227516928 | bytes 21495808 | tf_op jit(solution)/shard_map/dot_general | solution.py:16
  340.4 10.2 %fusion.139 = f32[256,512]{1,0:T(8,128)} fusion(bf16[4096,512]{1,0:T(8,128)(2,1)} %get-tuple-element.7, bf16[4096,512]{1,0:T(8,128)(2,1)} %get-tuple-element.4, bf16[256,4096]{0,1:T(8,128)(2,1)} %get-tuple-element.16, bf16[256,4096]{0,1:T(8,128)(2,1)S(1)} %get-tuple-element.15), kind=kOutput, calls=%fused_computation.191 | convolution fusion | flops 3277848576 | bytes 13107200 | tf_op jit(solution)/shard_map/dot_general | solution.py:81
  350.6 18.4 %reduce-precision_convert_fusion.6 = (bf16[256,4096]{0,1:T(8,128)(2,1)}, bf16[256,4096]{0,1:T(8,128)(2,1)}) fusion(f32[4096,256]{1,0:T(8,128)} %fusion.153, f32[512,256]{0,1:T(8,128)S(1)} %bitcast.181, f32[1,512,4096]{2,0,1:T(1,128)} %all-gather.9.cloned.1.call-done, f32[1,256,4096]{1,2,0:T(8,128)} %copy.74), kind=kOutput, calls=%fused_computation.37 | convolution fusion | flops 3227516928 | bytes 21495808 | tf_op jit(solution)/shard_map/dot_general | solution.py:16
  369.1 10.7 %fusion.138 = f32[256,512]{1,0:T(8,128)} fusion(bf16[4096,512]{1,0:T(8,128)(2,1)} %get-tuple-element.7, bf16[4096,512]{1,0:T(8,128)(2,1)} %get-tuple-element.4, bf16[256,4096]{0,1:T(8,128)(2,1)} %get-tuple-element.20, bf16[256,4096]{0,1:T(8,128)(2,1)} %get-tuple-element.19), kind=kOutput, calls=%fused_computation.190 | convolution fusion | flops 3277848576 | bytes 13107200 | tf_op jit(solution)/shard_map/dot_general | solution.py:81
  379.8 9.4 %fusion.135 = f32[256,512]{1,0:T(8,128)} fusion(bf16[4096,512]{1,0:T(8,128)(2,1)} %get-tuple-element.10, bf16[4096,512]{1,0:T(8,128)(2,1)} %get-tuple-element.5, bf16[256,4096]{0,1:T(8,128)(2,1)} %get-tuple-element.16, bf16[256,4096]{0,1:T(8,128)(2,1)S(1)} %get-tuple-element.15), kind=kOutput, calls=%fused_computation.187 | convolution fusion | flops 3277848576 | bytes 13107200 | tf_op jit(solution)/shard_map/dot_general | solution.py:81
  389.2 10.8 %fusion.134 = f32[256,512]{1,0:T(8,128)} fusion(bf16[4096,512]{1,0:T(8,128)(2,1)} %get-tuple-element.10, bf16[4096,512]{1,0:T(8,128)(2,1)} %get-tuple-element.5, bf16[256,4096]{0,1:T(8,128)(2,1)} %get-tuple-element.20, bf16[256,4096]{0,1:T(8,128)(2,1)} %get-tuple-element.19), kind=kOutput, calls=%fused_computation.186 | convolution fusion | flops 3277848576 | bytes 13107200 | tf_op jit(solution)/shard_map/dot_general | solution.py:81
  400.0 26.0 %fusion.140 = f32[512,512]{1,0:T(8,128)} fusion(bf16[4096,512]{1,0:T(8,128)(2,1)} %get-tuple-element.7, bf16[4096,512]{1,0:T(8,128)(2,1)} %get-tuple-element.4, bf16[512,4096]{0,1:T(8,128)(2,1)} %get-tuple-element.14, bf16[512,4096]{0,1:T(8,128)(2,1)} %get-tuple-element.13), kind=kOutput, calls=%fused_computation.192 | convolution fusion | flops 6517948416 | bytes 17825792 | tf_op jit(solution)/shard_map/dot_general | solution.py:81
  426.0 26.0 %fusion.136 = f32[512,512]{1,0:T(8,128)} fusion(bf16[4096,512]{1,0:T(8,128)(2,1)} %get-tuple-element.10, bf16[4096,512]{1,0:T(8,128)(2,1)} %get-tuple-element.5, bf16[512,4096]{0,1:T(8,128)(2,1)} %get-tuple-element.14, bf16[512,4096]{0,1:T(8,128)(2,1)} %get-tuple-element.13), kind=kOutput, calls=%fused_computation.188 | convolution fusion | flops 6517948416 | bytes 17825792 | tf_op jit(solution)/shard_map/dot_general | solution.py:81
  452.0 12.9 %reduce-precision_convert_fusion.5 = (bf16[512,4096]{1,0:T(8,128)(2,1)}, bf16[512,4096]{1,0:T(8,128)(2,1)}) fusion(f32[1,512,4096]{2,0,1:T(1,128)} %all-gather.9.cloned.1.call-done), kind=kLoop, calls=%fused_computation.17 | loop fusion | flops 8388608 | bytes 16777216 | tf_op jit(solution)/shard_map/convert_element_type | solution.py:23
  464.9 20.0 %fusion.141 = f32[512,512]{1,0:T(8,128)} fusion(bf16[4096,512]{1,0:T(8,128)(2,1)} %get-tuple-element.7, bf16[4096,512]{1,0:T(8,128)(2,1)} %get-tuple-element.4, bf16[512,4096]{1,0:T(8,128)(2,1)} %get-tuple-element.12, bf16[512,4096]{1,0:T(8,128)(2,1)} %get-tuple-element.11), kind=kOutput, calls=%fused_computation.193 | convolution fusion | flops 6517948416 | bytes 17825792 | tf_op jit(solution)/shard_map/dot_general | solution.py:81
  484.9 20.6 %fusion.137 = f32[512,512]{1,0:T(8,128)} fusion(bf16[4096,512]{1,0:T(8,128)(2,1)} %get-tuple-element.10, bf16[4096,512]{1,0:T(8,128)(2,1)} %get-tuple-element.5, bf16[512,4096]{1,0:T(8,128)(2,1)} %get-tuple-element.12, bf16[512,4096]{1,0:T(8,128)(2,1)} %get-tuple-element.11), kind=kOutput, calls=%fused_computation.189 | convolution fusion | flops 6517948416 | bytes 17825792 | tf_op jit(solution)/shard_map/dot_general | solution.py:81
  505.5 9.4 %fusion.130 = f32[256,512]{1,0:T(8,128)} fusion(bf16[4096,512]{1,0:T(8,128)(2,1)} %get-tuple-element.9, bf16[4096,512]{1,0:T(8,128)(2,1)} %get-tuple-element.6, bf16[256,4096]{0,1:T(8,128)(2,1)} %get-tuple-element.20, bf16[256,4096]{0,1:T(8,128)(2,1)S(1)} %copy-done.26), kind=kOutput, calls=%fused_computation.182 | convolution fusion | flops 3277848576 | bytes 13107200 | tf_op jit(solution)/shard_map/dot_general | solution.py:81
  515.0 26.0 %fusion.132 = f32[512,512]{1,0:T(8,128)} fusion(bf16[4096,512]{1,0:T(8,128)(2,1)} %get-tuple-element.9, bf16[4096,512]{1,0:T(8,128)(2,1)} %get-tuple-element.6, bf16[512,4096]{0,1:T(8,128)(2,1)} %get-tuple-element.14, bf16[512,4096]{0,1:T(8,128)(2,1)} %get-tuple-element.13), kind=kOutput, calls=%fused_computation.184 | convolution fusion | flops 6517948416 | bytes 17825792 | tf_op jit(solution)/shard_map/dot_general | solution.py:81
  540.9 20.5 %fusion.133 = f32[512,512]{1,0:T(8,128)} fusion(bf16[4096,512]{1,0:T(8,128)(2,1)} %get-tuple-element.9, bf16[4096,512]{1,0:T(8,128)(2,1)} %get-tuple-element.6, bf16[512,4096]{1,0:T(8,128)(2,1)} %get-tuple-element.12, bf16[512,4096]{1,0:T(8,128)(2,1)} %get-tuple-element.11), kind=kOutput, calls=%fused_computation.185 | convolution fusion | flops 6517948416 | bytes 17825792 | tf_op jit(solution)/shard_map/dot_general | solution.py:81
  561.5 2.5 collective-permute-start.11
  565.0 9.6 %fusion.131 = f32[256,512]{1,0:T(8,128)} fusion(bf16[4096,512]{1,0:T(8,128)(2,1)} %get-tuple-element.9, bf16[4096,512]{1,0:T(8,128)(2,1)} %get-tuple-element.6, bf16[256,4096]{0,1:T(8,128)(2,1)} %get-tuple-element.16, bf16[256,4096]{0,1:T(8,128)(2,1)S(1)} %copy-done.17), kind=kOutput, calls=%fused_computation.183 | convolution fusion | flops 3277848576 | bytes 13107200 | tf_op jit(solution)/shard_map/dot_general | solution.py:81
  579.1 9.8 %collective-permute-done.10 = f32[256,512]{1,0:T(8,128)} collective-permute-done((f32[256,512]{1,0:T(8,128)}, f32[256,512]{1,0:T(8,128)}, u32[]{:S(2)}, u32[]{:S(2)}) %collective-permute-start.10) | collective-permute-done | bytes 524320 | tf_op jit(solution)/shard_map/ppermute | solution.py:27
  588.9 2.4 collective-permute-start.2
  591.8 11.2 %fusion.46 = f32[256,512]{1,0:T(8,128)} fusion(f32[256,512]{1,0:T(8,128)} %collective-permute-done.11, f32[256,512]{1,0:T(8,128)} %collective-permute-done.10, f32[256,512]{1,0:T(8,128)} %collective-permute-done.9, bf16[4096,512]{1,0:T(8,128)(2,1)} %get-tuple-element.8, bf16[4096,512]{1,0:T(8,128)(2,1)} %get-tuple-element.3, ...), kind=kOutput, calls=%fused_computation.69 | convolution fusion | flops 3278372864 | bytes 14680064 | tf_op jit(solution)/shard_map/dot_general | solution.py:81
  603.0 3.5 all-to-all-start.6
  608.1 3.2 collective-permute-done.7
  612.9 9.8 %fusion.49 = f32[256,512]{1,0:T(8,128)} fusion(f32[256,512]{1,0:T(8,128)} %collective-permute-done.8, f32[256,512]{1,0:T(8,128)} %collective-permute-done.7, f32[256,512]{1,0:T(8,128)} %collective-permute-done.6, bf16[4096,512]{1,0:T(8,128)(2,1)} %get-tuple-element.8, bf16[4096,512]{1,0:T(8,128)(2,1)} %get-tuple-element.3, ...), kind=kOutput, calls=%fused_computation.73 | convolution fusion | flops 3278372864 | bytes 14680064 | tf_op jit(solution)/shard_map/dot_general | solution.py:81
  622.6 11.2 %collective-permute-done.2 = f32[512,512]{1,0:T(8,128)} collective-permute-done((f32[512,512]{1,0:T(8,128)}, f32[512,512]{1,0:T(8,128)}, u32[]{:S(2)}, u32[]{:S(2)}) %collective-permute-start.2) | collective-permute-done | bytes 1048608 | tf_op jit(solution)/shard_map/ppermute | solution.py:27
  635.4 3.5 all-to-all-start.4
  638.9 39.2 %collective-permute-done.1 = f32[512,512]{1,0:T(8,128)} collective-permute-done((f32[512,512]{1,0:T(8,128)}, f32[512,512]{1,0:T(8,128)}, u32[]{:S(2)}, u32[]{:S(2)}) %collective-permute-start.1) | collective-permute-done | bytes 1048608 | tf_op jit(solution)/shard_map/ppermute | solution.py:27
  678.8 21.2 %fusion.40 = f32[512,512]{1,0:T(8,128)} fusion(f32[512,512]{1,0:T(8,128)} %collective-permute-done.2, f32[512,512]{1,0:T(8,128)} %collective-permute-done.1, f32[512,512]{1,0:T(8,128)} %collective-permute-done, bf16[4096,512]{1,0:T(8,128)(2,1)} %get-tuple-element.8, bf16[4096,512]{1,0:T(8,128)(2,1)} %get-tuple-element.3, ...), kind=kOutput, calls=%fused_computation.62 | convolution fusion | flops 6518996992 | bytes 20971520 | tf_op jit(solution)/shard_map/dot_general | solution.py:81
  701.2 3.6 all-to-all-start.7
  704.9 26.6 %fusion.43 = f32[512,512]{1,0:T(8,128)} fusion(f32[512,512]{1,0:T(8,128)} %collective-permute-done.5, f32[512,512]{1,0:T(8,128)} %collective-permute-done.4, f32[512,512]{1,0:T(8,128)S(1)} %collective-permute-done.3, bf16[4096,512]{1,0:T(8,128)(2,1)} %get-tuple-element.8, bf16[4096,512]{1,0:T(8,128)(2,1)} %get-tuple-element.3, ...), kind=kOutput, calls=%fused_computation.65 | convolution fusion | flops 6518996992 | bytes 20971520 | tf_op jit(solution)/shard_map/dot_general | solution.py:81
  732.7 4.2 all-to-all-start.5
  737.7 6.3 all-to-all-done.5
  744.0 3.6 all-to-all-start
  747.6 3.6 fusion.73
  757.8 16.3 %all-to-all-done = f32[8,64,512]{2,1,0:T(8,128)S(1)} async-done(((f32[8,64,512]{2,1,0:T(8,128)}), f32[8,64,512]{2,1,0:T(8,128)S(1)}, u32[]{:S(2)}, u32[]{:S(2)}) %all-to-all-start) | async-done | bytes 1048608 | tf_op jit(solution)/shard_map/all_to_all | solution.py:88
  774.1 4.5 all-to-all-start.2
  778.6 3.6 fusion.75
  791.9 3.0 copy.62
  794.9 10.3 %all-to-all-done.2 = f32[8,64,512]{2,1,0:T(8,128)} async-done(((f32[8,64,512]{2,1,0:T(8,128)}), f32[8,64,512]{2,1,0:T(8,128)}, u32[]{:S(2)}, u32[]{:S(2)}) %all-to-all-start.2) | async-done | bytes 1048608 | tf_op jit(solution)/shard_map/all_to_all | solution.py:88
  805.1 4.3 all-to-all-start.1
  818.4 3.0 copy.66
  823.2 4.2 all-to-all-start.3
  830.6 2.9 neg.35
  835.7 8.2 fusion.129
  844.0 3.6 fusion.128
  847.6 2.5 fusion.127
  858.8 2.9 neg.37
  863.2 6.3 fusion.81
  880.2 2.9 stack_reshape.6
  886.2 2.9 stack_reshape.7
  889.2 3.9 maximum_bitcast_fusion
  (236 shorter events, 113.9 us)
Async XLA Ops:
  7.2 64.2 %all-gather.13.cloned.1.call-start = ((), (), s32[]{:S(2)}) async-start(), calls=%async_computation.10 | async-start | bytes 4718592 | tf_op jit(solution)/shard_map/all_gather | solution.py:48
  14.2 10.6 %copy-start = (f32[3,512,512]{2,1,0:T(8,128)S(1)}, f32[3,512,512]{2,1,0:T(8,128)}, u32[]{:S(2)}) copy-start(f32[3,512,512]{2,1,0:T(8,128)} %param.8) | copy-start | bytes 9437188
  16.3 97.5 %all-gather.15.cloned.1.call-start = ((), (), s32[]{:S(2)}) async-start(), calls=%async_computation.11 | async-start | bytes 4718592 | tf_op jit(solution)/shard_map/all_gather | solution.py:48
  17.1 179.2 %all-gather.11.cloned.1.call-start = ((), (), s32[]{:S(2)}) async-start(), calls=%async_computation.9 | async-start | bytes 9437184 | tf_op jit(solution)/shard_map/all_gather | solution.py:48
  24.2 254.7 %all-gather.9.cloned.1.call-start = ((), (), s32[]{:S(2)}) async-start(), calls=%async_computation.8 | async-start | bytes 9437184 | tf_op jit(solution)/shard_map/all_gather | solution.py:48
  31.7 5.4 copy-start.5
  31.7 6.2 copy-start.7
  33.9 5.4 copy-start.33
  37.1 8.5 copy-start.2
  37.9 7.8 copy-start.6
  278.9 37.5 %copy-start.15 = (f32[512,8,32]{0,2,1:T(8,128)S(1)}, f32[512,8,32]{0,2,1:T(8,128)}, u32[]{:S(2)}) copy-start(f32[512,8,32]{0,2,1:T(8,128)} %get-tuple-element.36) | copy-start | bytes 1572868
  316.4 5.1 copy-start.14
  340.4 39.4 %copy-start.16 = (bf16[256,4096]{0,1:T(8,128)(2,1)}, bf16[256,4096]{0,1:T(8,128)(2,1)S(1)}, u32[]{:S(2)}) copy-start(bf16[256,4096]{0,1:T(8,128)(2,1)S(1)} %get-tuple-element.15) | copy-start | bytes 6291460
  340.4 10.2 %copy-start.31 = (f32[512,8,32]{0,2,1:T(8,128)S(1)}, f32[512,8,32]{0,2,1:T(8,128)}, u32[]{:S(2)}) copy-start(f32[512,8,32]{0,2,1:T(8,128)} %get-tuple-element.34) | copy-start | bytes 1572868
  484.9 20.6 %copy-start.26 = (bf16[256,4096]{0,1:T(8,128)(2,1)S(1)}, bf16[256,4096]{0,1:T(8,128)(2,1)}, u32[]{:S(2)}) copy-start(bf16[256,4096]{0,1:T(8,128)(2,1)} %get-tuple-element.19) | copy-start | bytes 6291460
  540.9 23.6 %copy-start.53 = (f32[256,512]{1,0:T(8,128)S(1)}, f32[256,512]{1,0:T(8,128)}, u32[]{:S(2)}) copy-start(f32[256,512]{1,0:T(8,128)} %fusion.138) | copy-start | bytes 1572868
  540.9 24.1 %copy-start.17 = (bf16[256,4096]{0,1:T(8,128)(2,1)S(1)}, bf16[256,4096]{0,1:T(8,128)(2,1)}, u32[]{:S(2)}) copy-start(bf16[256,4096]{0,1:T(8,128)(2,1)} %copy-done.16) | copy-start | bytes 6291460
  561.5 16.1 %copy-start.52 = (f32[256,512]{1,0:T(8,128)S(1)}, f32[256,512]{1,0:T(8,128)}, u32[]{:S(2)}) copy-start(f32[256,512]{1,0:T(8,128)} %fusion.139) | copy-start | bytes 1572868
  561.5 16.1 %collective-permute-start.11 = (f32[256,512]{1,0:T(8,128)}, f32[256,512]{1,0:T(8,128)}, u32[]{:S(2)}, u32[]{:S(2)}) collective-permute-start(f32[256,512]{1,0:T(8,128)} %fusion.130), channel_id=1, source_target_pairs={{0,24},{8,16},{16,8},{24,0},{1,25},{9,17},{17,9},{25,1},{2,26},{10... | collective-permute-start | bytes 1572872 | tf_op jit(solution)/shard_map/ppermute | solution.py:27
  564.0 24.9 %collective-permute-start.10 = (f32[256,512]{1,0:T(8,128)}, f32[256,512]{1,0:T(8,128)}, u32[]{:S(2)}, u32[]{:S(2)}) collective-permute-start(f32[256,512]{1,0:T(8,128)} %fusion.134), channel_id=1, source_target_pairs={{0,16},{8,24},{16,0},{24,8},{1,17},{9,25},{17,1},{25,9},{2,18},{10... | collective-permute-start | bytes 1572872 | tf_op jit(solution)/shard_map/ppermute | solution.py:27
  564.5 26.8 %collective-permute-start.9 = (f32[256,512]{1,0:T(8,128)S(1)}, f32[256,512]{1,0:T(8,128)}, u32[]{:S(2)}, u32[]{:S(2)}) collective-permute-start(f32[256,512]{1,0:T(8,128)S(1)} %copy-done.53), channel_id=1, source_target_pairs={{0,8},{8,0},{16,24},{24,16},{1,9},{9,1},{17,25},{25,17},{2,10},{10... | collective-permute-start | bytes 1572872 | tf_op jit(solution)/shard_map/ppermute | solution.py:27
  574.6 31.9 %collective-permute-start.8 = (f32[256,512]{1,0:T(8,128)}, f32[256,512]{1,0:T(8,128)}, u32[]{:S(2)}, u32[]{:S(2)}) collective-permute-start(f32[256,512]{1,0:T(8,128)} %fusion.131), channel_id=1, source_target_pairs={{0,24},{8,16},{16,8},{24,0},{1,25},{9,17},{17,9},{25,1},{2,26},{10... | collective-permute-start | bytes 1572872 | tf_op jit(solution)/shard_map/ppermute | solution.py:27
  577.0 34.3 %collective-permute-start.7 = (f32[256,512]{1,0:T(8,128)}, f32[256,512]{1,0:T(8,128)}, u32[]{:S(2)}, u32[]{:S(2)}) collective-permute-start(f32[256,512]{1,0:T(8,128)} %fusion.135), channel_id=1, source_target_pairs={{0,16},{8,24},{16,0},{24,8},{1,17},{9,25},{17,1},{25,9},{2,18},{10... | collective-permute-start | bytes 1572872 | tf_op jit(solution)/shard_map/ppermute | solution.py:27
  577.6 35.2 %collective-permute-start.6 = (f32[256,512]{1,0:T(8,128)S(1)}, f32[256,512]{1,0:T(8,128)}, u32[]{:S(2)}, u32[]{:S(2)}) collective-permute-start(f32[256,512]{1,0:T(8,128)S(1)} %copy-done.52), channel_id=1, source_target_pairs={{0,8},{8,0},{16,24},{24,16},{1,9},{9,1},{17,25},{25,17},{2,10},{10... | collective-permute-start | bytes 1572872 | tf_op jit(solution)/shard_map/ppermute | solution.py:27
  588.9 45.0 %collective-permute-start.2 = (f32[512,512]{1,0:T(8,128)}, f32[512,512]{1,0:T(8,128)}, u32[]{:S(2)}, u32[]{:S(2)}) collective-permute-start(f32[512,512]{1,0:T(8,128)} %fusion.133), channel_id=1, source_target_pairs={{0,24},{8,16},{16,8},{24,0},{1,25},{9,17},{17,9},{25,1},{2,26},{10... | collective-permute-start | bytes 3145736 | tf_op jit(solution)/shard_map/ppermute | solution.py:27
  591.3 113.6 %collective-permute-start.5 = (f32[512,512]{1,0:T(8,128)}, f32[512,512]{1,0:T(8,128)}, u32[]{:S(2)}, u32[]{:S(2)}) collective-permute-start(f32[512,512]{1,0:T(8,128)} %fusion.132), channel_id=1, source_target_pairs={{0,24},{8,16},{16,8},{24,0},{1,25},{9,17},{17,9},{25,1},{2,26},{10... | collective-permute-start | bytes 3145736 | tf_op jit(solution)/shard_map/ppermute | solution.py:27
  603.0 32.4 %all-to-all-start.6 = ((f32[8,32,512]{2,1,0:T(8,128)}), f32[8,32,512]{2,1,0:T(8,128)S(1)}, u32[]{:S(2)}, u32[]{:S(2)}) async-start(f32[8,32,512]{2,1,0:T(8,128)} %bitcast.23), calls=%async_computation.6 | async-start | bytes 1048576 | tf_op jit(solution)/shard_map/all_to_all | solution.py:88
  606.5 71.5 %collective-permute-start.1 = (f32[512,512]{1,0:T(8,128)}, f32[512,512]{1,0:T(8,128)}, u32[]{:S(2)}, u32[]{:S(2)}) collective-permute-start(f32[512,512]{1,0:T(8,128)} %fusion.137), channel_id=1, source_target_pairs={{0,16},{8,24},{16,0},{24,8},{1,17},{9,25},{17,1},{25,9},{2,18},{10... | collective-permute-start | bytes 3145736 | tf_op jit(solution)/shard_map/ppermute | solution.py:27
  611.3 93.5 %collective-permute-start.4 = (f32[512,512]{1,0:T(8,128)}, f32[512,512]{1,0:T(8,128)}, u32[]{:S(2)}, u32[]{:S(2)}) collective-permute-start(f32[512,512]{1,0:T(8,128)} %fusion.136), channel_id=1, source_target_pairs={{0,16},{8,24},{16,0},{24,8},{1,17},{9,25},{17,1},{25,9},{2,18},{10... | collective-permute-start | bytes 3145736 | tf_op jit(solution)/shard_map/ppermute | solution.py:27
  612.8 66.0 %collective-permute-start = (f32[512,512]{1,0:T(8,128)}, f32[512,512]{1,0:T(8,128)}, u32[]{:S(2)}, u32[]{:S(2)}) collective-permute-start(f32[512,512]{1,0:T(8,128)} %fusion.141), channel_id=1, source_target_pairs={{0,8},{8,0},{16,24},{24,16},{1,9},{9,1},{17,25},{25,17},{2,10},{10... | collective-permute-start | bytes 3145736 | tf_op jit(solution)/shard_map/ppermute | solution.py:27
  633.9 71.0 %collective-permute-start.3 = (f32[512,512]{1,0:T(8,128)}, f32[512,512]{1,0:T(8,128)S(1)}, u32[]{:S(2)}, u32[]{:S(2)}) collective-permute-start(f32[512,512]{1,0:T(8,128)} %fusion.140), channel_id=1, source_target_pairs={{0,8},{8,0},{16,24},{24,16},{1,9},{9,1},{17,25},{25,17},{2,10},{10... | collective-permute-start | bytes 3145736 | tf_op jit(solution)/shard_map/ppermute | solution.py:27
  635.4 65.8 %all-to-all-start.4 = ((f32[8,32,512]{2,1,0:T(8,128)}), f32[8,32,512]{2,1,0:T(8,128)S(1)}, u32[]{:S(2)}, u32[]{:S(2)}) async-start(f32[8,32,512]{2,1,0:T(8,128)} %bitcast.16), calls=%async_computation.4 | async-start | bytes 1048576 | tf_op jit(solution)/shard_map/all_to_all | solution.py:88
  701.2 31.5 %all-to-all-start.7 = ((f32[4,2,32,512]{3,1,2,0:T(2,128)}), f32[4,2,32,512]{3,1,2,0:T(2,128)S(1)}, u32[]{:S(2)}, u32[]{:S(2)}) async-start(f32[4,2,32,512]{3,1,2,0:T(2,128)} %copy.75), calls=%async_computation.7 | async-start | bytes 1048576 | tf_op jit(solution)/shard_map/all_to_all | solution.py:89
  732.7 11.3 %all-to-all-start.5 = ((f32[4,2,32,512]{3,1,2,0:T(2,128)}), f32[4,2,32,512]{3,1,2,0:T(2,128)S(1)}, u32[]{:S(2)}, u32[]{:S(2)}) async-start(f32[4,2,32,512]{3,1,2,0:T(2,128)} %copy.72), calls=%async_computation.5 | async-start | bytes 1048576 | tf_op jit(solution)/shard_map/all_to_all | solution.py:89
  737.6 13.6 %copy-start.8 = (f32[32,4096]{1,0:T(8,128)}, f32[32,4096]{1,0:T(8,128)S(1)}, u32[]{:S(2)}) copy-start(f32[32,4096]{1,0:T(8,128)S(1)} %reshape.107) | copy-start | bytes 1572868
  744.0 30.1 %all-to-all-start = ((f32[8,64,512]{2,1,0:T(8,128)}), f32[8,64,512]{2,1,0:T(8,128)S(1)}, u32[]{:S(2)}, u32[]{:S(2)}) async-start(f32[8,64,512]{2,1,0:T(8,128)} %bitcast.1), calls=%async_computation | async-start | bytes 2097152 | tf_op jit(solution)/shard_map/all_to_all | solution.py:88
  753.5 36.2 %collective-permute-start.22 = (f32[32,512]{1,0:T(8,128)}, f32[32,512]{1,0:T(8,128)S(1)}, u32[]{:S(2)}, u32[]{:S(2)}) collective-permute-start(f32[32,512]{1,0:T(8,128)} %pad_maximum_fusion.28), channel_id=1, source_target_pairs={{0,16},{8,24},{16,0},{24,8},{1,17},{9,25},{17,1},{25,9},{2,18},{10... | collective-permute-start | bytes 196616 | tf_op jit(solution)/shard_map/ppermute | solution.py:27
  754.9 35.3 %collective-permute-start.23 = (f32[32,512]{1,0:T(8,128)}, f32[32,512]{1,0:T(8,128)S(1)}, u32[]{:S(2)}, u32[]{:S(2)}) collective-permute-start(f32[32,512]{1,0:T(8,128)} %pad_maximum_fusion.28), channel_id=1, source_target_pairs={{0,24},{8,16},{16,8},{24,0},{1,25},{9,17},{17,9},{25,1},{2,26},{10... | collective-permute-start | bytes 196616 | tf_op jit(solution)/shard_map/ppermute | solution.py:27
  756.4 33.9 %collective-permute-start.21 = (f32[32,512]{1,0:T(8,128)}, f32[32,512]{1,0:T(8,128)S(1)}, u32[]{:S(2)}, u32[]{:S(2)}) collective-permute-start(f32[32,512]{1,0:T(8,128)} %pad_maximum_fusion.28), channel_id=1, source_target_pairs={{0,8},{8,0},{16,24},{24,16},{1,9},{9,1},{17,25},{25,17},{2,10},{10... | collective-permute-start | bytes 196616 | tf_op jit(solution)/shard_map/ppermute | solution.py:27
  757.7 24.5 %copy-start.10 = (f32[32,4096]{1,0:T(8,128)}, f32[32,4096]{1,0:T(8,128)S(1)}, u32[]{:S(2)}) copy-start(f32[32,4096]{1,0:T(8,128)S(1)} %reshape.102) | copy-start | bytes 1572868
  774.1 8.1 copy-start.13
  774.1 31.1 %all-to-all-start.2 = ((f32[8,64,512]{2,1,0:T(8,128)}), f32[8,64,512]{2,1,0:T(8,128)}, u32[]{:S(2)}, u32[]{:S(2)}) async-start(f32[8,64,512]{2,1,0:T(8,128)} %bitcast.183), calls=%async_computation.2 | async-start | bytes 2097152 | tf_op jit(solution)/shard_map/all_to_all | solution.py:88
  783.8 7.1 copy-start.51
  783.9 32.2 %copy-start.1 = (f32[3,512,512]{2,1,0:T(8,128)S(1)}, f32[3,512,512]{2,1,0:T(8,128)}, u32[]{:S(2)}) copy-start(f32[3,512,512]{2,1,0:T(8,128)} %param.8) | copy-start | bytes 9437188
  783.9 32.2 %copy-start.35 = (f32[64,512]{1,0:T(8,128)S(1)}, f32[64,512]{1,0:T(8,128)}, u32[]{:S(2)}) copy-start(f32[64,512]{1,0:T(8,128)} %fusion.60) | copy-start | bytes 393220
  786.8 25.0 %collective-permute-start.19 = (f32[32,512]{1,0:T(8,128)}, f32[32,512]{1,0:T(8,128)}, u32[]{:S(2)}, u32[]{:S(2)}) collective-permute-start(f32[32,512]{1,0:T(8,128)} %pad_maximum_fusion.27), channel_id=1, source_target_pairs={{0,16},{8,24},{16,0},{24,8},{1,17},{9,25},{17,1},{25,9},{2,18},{10... | collective-permute-start | bytes 196616 | tf_op jit(solution)/shard_map/ppermute | solution.py:27
  788.2 23.6 %collective-permute-start.20 = (f32[32,512]{1,0:T(8,128)}, f32[32,512]{1,0:T(8,128)}, u32[]{:S(2)}, u32[]{:S(2)}) collective-permute-start(f32[32,512]{1,0:T(8,128)} %pad_maximum_fusion.27), channel_id=1, source_target_pairs={{0,24},{8,16},{16,8},{24,0},{1,25},{9,17},{17,9},{25,1},{2,26},{10... | collective-permute-start | bytes 196616 | tf_op jit(solution)/shard_map/ppermute | solution.py:27
  789.7 22.1 %collective-permute-start.18 = (f32[32,512]{1,0:T(8,128)}, f32[32,512]{1,0:T(8,128)}, u32[]{:S(2)}, u32[]{:S(2)}) collective-permute-start(f32[32,512]{1,0:T(8,128)} %pad_maximum_fusion.27), channel_id=1, source_target_pairs={{0,8},{8,0},{16,24},{24,16},{1,9},{9,1},{17,25},{25,17},{2,10},{10... | collective-permute-start | bytes 196616 | tf_op jit(solution)/shard_map/ppermute | solution.py:27
  805.1 18.1 %all-to-all-start.1 = ((f32[4,2,64,512]{3,1,2,0:T(2,128)}), f32[4,2,64,512]{3,1,2,0:T(2,128)}, u32[]{:S(2)}, u32[]{:S(2)}) async-start(f32[4,2,64,512]{3,1,2,0:T(2,128)} %copy.62), calls=%async_computation.1 | async-start | bytes 2097152 | tf_op jit(solution)/shard_map/all_to_all | solution.py:89
  823.2 32.5 %all-to-all-start.3 = ((f32[4,2,64,512]{3,1,2,0:T(2,128)}), f32[4,2,64,512]{3,1,2,0:T(2,128)}, u32[]{:S(2)}, u32[]{:S(2)}) async-start(f32[4,2,64,512]{3,1,2,0:T(2,128)} %copy.66), calls=%async_computation.3 | async-start | bytes 2097152 | tf_op jit(solution)/shard_map/all_to_all | solution.py:89
  835.7 8.2 copy-start.11
  835.7 8.3 copy-start.12
  843.9 7.5 copy-start.41
  852.3 54.1 %collective-permute-start.13 = (f32[64,1536]{1,0:T(8,128)}, f32[64,1536]{1,0:T(8,128)}, u32[]{:S(2)}, u32[]{:S(2)}) collective-permute-start(f32[64,1536]{1,0:T(8,128)} %pad_maximum_fusion.16), channel_id=1, source_target_pairs={{0,16},{8,24},{16,0},{24,8},{1,17},{9,25},{17,1},{25,9},{2,18},{10... | collective-permute-start | bytes 1179656 | tf_op jit(solution)/shard_map/ppermute | solution.py:27
  854.2 52.1 %collective-permute-start.14 = (f32[64,1536]{1,0:T(8,128)}, f32[64,1536]{1,0:T(8,128)}, u32[]{:S(2)}, u32[]{:S(2)}) collective-permute-start(f32[64,1536]{1,0:T(8,128)} %pad_maximum_fusion.16), channel_id=1, source_target_pairs={{0,24},{8,16},{16,8},{24,0},{1,25},{9,17},{17,9},{25,1},{2,26},{10... | collective-permute-start | bytes 1179656 | tf_op jit(solution)/shard_map/ppermute | solution.py:27
  863.2 6.3 copy-start.21
  863.2 6.3 copy-start.25
  873.7 19.4 %collective-permute-start.16 = (f32[64,1024]{1,0:T(8,128)}, f32[64,1024]{1,0:T(8,128)S(1)}, u32[]{:S(2)}, u32[]{:S(2)}) collective-permute-start(f32[64,1024]{1,0:T(8,128)} %pad_maximum_fusion.20), channel_id=1, source_target_pairs={{0,16},{8,24},{16,0},{24,8},{1,17},{9,25},{17,1},{25,9},{2,18},{10... | collective-permute-start | bytes 786440 | tf_op jit(solution)/shard_map/ppermute | solution.py:27
  875.1 18.0 %collective-permute-start.17 = (f32[64,1024]{1,0:T(8,128)}, f32[64,1024]{1,0:T(8,128)}, u32[]{:S(2)}, u32[]{:S(2)}) collective-permute-start(f32[64,1024]{1,0:T(8,128)} %pad_maximum_fusion.20), channel_id=1, source_target_pairs={{0,24},{8,16},{16,8},{24,0},{1,25},{9,17},{17,9},{25,1},{2,26},{10... | collective-permute-start | bytes 786440 | tf_op jit(solution)/shard_map/ppermute | solution.py:27
  875.2 18.6 %collective-permute-start.15 = (f32[64,1024]{1,0:T(8,128)}, f32[64,1024]{1,0:T(8,128)}, u32[]{:S(2)}, u32[]{:S(2)}) collective-permute-start(f32[64,1024]{1,0:T(8,128)} %pad_maximum_fusion.20), channel_id=1, source_target_pairs={{0,8},{8,0},{16,24},{24,16},{1,9},{9,1},{17,25},{25,17},{2,10},{10... | collective-permute-start | bytes 786440 | tf_op jit(solution)/shard_map/ppermute | solution.py:27
  884.6 17.6 %copy-start.34 = (f32[64,512]{1,0:T(8,128)S(1)}, f32[64,512]{1,0:T(8,128)}, u32[]{:S(2)}) copy-start(f32[64,512]{1,0:T(8,128)} %copy-done.33) | copy-start | bytes 393220
  893.0 13.3 %collective-permute-start.12 = (f32[64,1536]{1,0:T(8,128)}, f32[64,1536]{1,0:T(8,128)}, u32[]{:S(2)}, u32[]{:S(2)}) collective-permute-start(f32[64,1536]{1,0:T(8,128)} %pad_maximum_fusion.16), channel_id=1, source_target_pairs={{0,8},{8,0},{16,24},{24,16},{1,9},{9,1},{17,25},{25,17},{2,10},{10... | collective-permute-start | bytes 1179656 | tf_op jit(solution)/shard_map/ppermute | solution.py:27
  904.5 10.0 %copy-start.36 = (f32[1,64,512]{2,1,0:T(8,128)S(1)}, f32[1,64,512]{2,1,0:T(8,128)}, u32[]{:S(2)}) copy-start(f32[1,64,512]{2,1,0:T(8,128)} %fusion.54) | copy-start | bytes 393220
  904.5 10.0 %copy-start.37 = (f32[1,64,512]{2,1,0:T(8,128)S(1)}, f32[1,64,512]{2,1,0:T(8,128)}, u32[]{:S(2)}) copy-start(f32[1,64,512]{2,1,0:T(8,128)} %fusion.82) | copy-start | bytes 393220
  (26 other events, 71.9 us)
Sparse Core Ops, SparseCore 0:
  16.4 49.8 all-gather.12
  67.9 45.8 all-gather.14
  115.4 80.7 all-gather.10
  198.2 80.5 all-gather.8

commit v2 on v1

v2 whole, which is shorter than its diff:
```python
import functools

import jax
import jax.numpy as jnp
from jax import lax
from jax.experimental import pallas as pl
from jax.experimental.pallas import tpu as pltpu
from jax.sharding import PartitionSpec as P

NB = 128
MIB = 1024 * 1024

precise = lax.Precision.HIGHEST


def matmul(left, right):
    return jnp.dot(left, right, precision=precise, preferred_element_type=jnp.float32)


def tdot(left, right):
    return lax.dot_general(
        left, right, (((0,), (0,)), ((), ())), precision=precise, preferred_element_type=jnp.float32
    )


def tile_of(size, wanted):
    return wanted if size % wanted == 0 else size


def split(values):
    high = lax.reduce_precision(values, exponent_bits=8, mantissa_bits=7)
    return high.astype(jnp.bfloat16), (values - high).astype(jnp.bfloat16)


def split_here(values):
    high = values.astype(jnp.bfloat16)
    return high, (values - high.astype(jnp.float32)).astype(jnp.bfloat16)


def triple_dot(left_high, left_low, right_high, right_low):
    left = jnp.concatenate([left_high, left_high, left_low], 1)
    right = jnp.concatenate([right_high, right_low, right_high], 0)
    return jnp.dot(left, right, preferred_element_type=jnp.float32)


def params(limit):
    return pltpu.CompilerParams(vmem_limit_bytes=limit * MIB)


def cost(flops, bytes_accessed):
    return pl.CostEstimate(flops=flops, bytes_accessed=bytes_accessed, transcendentals=0)


def exchange(value, axis, size, step):
    return lax.ppermute(value, axis, [(i, i ^ step) for i in range(size)])


def mask_kernel(panel_ref, mask_ref, token_ref, out_ref):
    out_ref[...] = panel_ref[0] * mask_ref[0]


def masked(panels, mask, token, j, lo, hi):
    rows = panels.shape[2]
    count = hi - lo
    return pl.pallas_call(
        mask_kernel,
        grid=(1,),
        out_shape=jax.ShapeDtypeStruct((count, rows), jnp.float32),
        in_specs=[
            pl.BlockSpec((1, count, rows), lambda i: (j, lo // count, 0)),
            pl.BlockSpec((1, 1, rows), lambda i: (j, 0, 0)),
            pl.BlockSpec(memory_space=pl.ANY),
        ],
        out_specs=pl.BlockSpec((count, rows), lambda i: (0, 0)),
        compiler_params=params(32),
        cost_estimate=cost(count * rows, 8 * count * rows),
        name="masked",
    )(panels, mask, token)


def prepare_kernel(order_ref, a_ref, token_ref, high_ref, low_ref):
    high_ref[0], low_ref[0] = split_here(a_ref[...])


def prepared(ainv, order, token, count, part):
    rows = ainv.shape[0]
    if part % 128:
        pieces = [
            split(lax.dynamic_slice_in_dim(ainv, order[s] * part, part, 1)) for s in range(count)
        ]
        return jnp.stack([p[0] for p in pieces], 0), jnp.stack([p[1] for p in pieces], 0)
    tile = tile_of(rows, 1024)
    shape = jax.ShapeDtypeStruct((count, rows, part), jnp.bfloat16)
    spec = pl.BlockSpec((1, tile, part), lambda s, i, order: (s, i, 0))
    return pl.pallas_call(
        prepare_kernel,
        out_shape=(shape, shape),
        grid_spec=pltpu.PrefetchScalarGridSpec(
            num_scalar_prefetch=1,
            grid=(count, rows // tile),
            in_specs=[
                pl.BlockSpec((tile, part), lambda s, i, order: (i, order[s])),
                pl.BlockSpec(memory_space=pl.ANY),
            ],
            out_specs=(spec, spec),
        ),
        compiler_params=params(32),
        cost_estimate=cost(4 * ainv.size, 8 * ainv.size),
        name="prepared",
    )(order, ainv, token)


def product_kernel(first, count, depth, with_pre, with_split, *refs):
    refs = list(refs)
    if with_split:
        gathered_ref = refs.pop(0)
        pre_ref = refs.pop(0) if with_pre else None
        a_high_ref, a_low_ref = refs.pop(0), refs.pop(0)
        high_ref, low_ref = refs.pop(0), refs.pop(0)
    else:
        high_ref, low_ref = refs.pop(0), refs.pop(0)
        a_high_ref, a_low_ref = refs.pop(0), refs.pop(0)
    outs, total_ref = refs[:count], refs[count]
    s, n = pl.program_id(0), pl.program_id(1)
    rows = high_ref.shape[0]

    if with_split:
        strip = 16

        @pl.when((s == 0) & (n == 0))
        def _():
            @pl.loop(0, rows // strip)
            def _(i):
                here = pl.ds(pl.multiple_of(i * strip, strip), strip)
                values = gathered_ref[here, :]
                if with_pre:
                    values = values - pre_ref[here, :]
                high_ref[here, :], low_ref[here, :] = split_here(values)

    steps = high_ref.shape[1] // depth

    @pl.loop(0, steps)
    def _(k):
        here = pl.ds(pl.multiple_of(k * depth, depth), depth)
        value = triple_dot(
            high_ref[:, here], low_ref[:, here], a_high_ref[0, here, :], a_low_ref[0, here, :]
        )

        @pl.when(k == 0)
        def _():
            total_ref[...] = value

        @pl.when(k > 0)
        def _():
            total_ref[...] += value

    for i in range(count):
        @pl.when(s == i)
        def _():
            outs[i][...] = total_ref[...]


def products(factor, inverse, first, last, pre=None):
    with_split = not isinstance(factor, tuple)
    a_high, a_low = inverse
    count = last - first
    part = a_high.shape[2]
    rows, depth_all = (factor if with_split else factor[0]).shape
    tile = tile_of(part, 256)
    tiles = part // tile
    once = pl.Buffered(1)
    whole = pl.BlockSpec((rows, depth_all), lambda s, n: (0, 0), pipeline_mode=once)
    a_spec = pl.BlockSpec((1, depth_all, tile), lambda s, n: (s + first, 0, n))

    def out_spec(i):
        return pl.BlockSpec(
            (rows, tile), lambda s, n: (0, jnp.where(s < i, 0, jnp.where(s > i, tiles - 1, n)))
        )

    out_shape = [jax.ShapeDtypeStruct((rows, part), jnp.float32)] * count
    out_specs = [out_spec(i) for i in range(count)]
    if with_split:
        operands = [factor] + ([] if pre is None else [pre]) + [a_high, a_low]
        in_specs = [whole] * (len(operands) - 2) + [a_spec, a_spec]
        out_shape = [jax.ShapeDtypeStruct((rows, depth_all), jnp.bfloat16)] * 2 + out_shape
        out_specs = [pl.BlockSpec((rows, depth_all), lambda s, n: (0, 0))] * 2 + out_specs
    else:
        operands = [factor[0], factor[1], a_high, a_low]
        in_specs = [whole, whole, a_spec, a_spec]
    got = pl.pallas_call(
        functools.partial(
            product_kernel, first, count, tile_of(depth_all, 1024), pre is not None, with_split
        ),
        grid=(count, tiles),
        out_shape=out_shape,
        in_specs=in_specs,
        out_specs=out_specs,
        scratch_shapes=[pltpu.VMEM((rows, tile), jnp.float32)],
        compiler_params=params(56),
        cost_estimate=cost(
            6 * rows * depth_all * part * count, 4 * depth_all * part * count + 8 * rows * depth_all
        ),
        name="products",
    )(*operands)
    if with_split:
        return (got[0], got[1]), list(got[2:])
    return factor, list(got)


def elimination_kernel(count, *refs):
    value = None
    for i in range(count):
        c_high, c_low, f_high, f_low = (r[...] for r in refs[4 * i : 4 * i + 4])
        term = triple_dot(c_high, c_low, f_high, f_low)
        value = term if value is None else value + term
    refs[-1][...] = value


def elimination(pairs):
    operands = []
    for coupled, (high, low) in pairs:
        operands += [*split(coupled), high, low]
    rows, depth = pairs[0][0].shape
    length = pairs[0][1][0].shape[1]
    tile = tile_of(length, 512)
    left = pl.BlockSpec((rows, depth), lambda i: (0, 0))
    right = pl.BlockSpec((depth, tile), lambda i: (0, i))
    return pl.pallas_call(
        functools.partial(elimination_kernel, len(pairs)),
        grid=(length // tile,),
        out_shape=jax.ShapeDtypeStruct((rows, length), jnp.float32),
        in_specs=[left, left, right, right] * len(pairs),
        out_specs=pl.BlockSpec((rows, tile), lambda i: (0, i)),
        compiler_params=params(48),
        cost_estimate=cost(
            6 * rows * depth * length * len(pairs), 4 * length * (rows + depth * len(pairs))
        ),
        name="elimination",
    )(*operands)


def inner_products(left, right):
    nt = (((1,), (1,)), ((), ()))
    high, low = split(left)
    rows = left.shape[0]
    both = lax.dot_general(
        jnp.concatenate([high, low], 0), right[0], nt, preferred_element_type=jnp.float32
    )
    cross = lax.dot_general(high, right[1], nt, preferred_element_type=jnp.float32)
    return both[:rows] + both[rows:] + cross


def shards(ainv, panels, pattern, coupling, dinv):
    rows_n = lax.axis_size("prow")
    cols_n = lax.axis_size("pcol")
    row = lax.axis_index("prow")
    col = lax.axis_index("pcol")
    local_rows, local_cols = panels.shape[1:]
    part = ainv.shape[1] // rows_n
    ratio = cols_n // rows_n
    blocks_here = local_rows // NB

    flags = lax.dynamic_slice_in_dim(pattern, row * blocks_here, blocks_here, 1)
    mask = jnp.repeat(flags.astype(jnp.float32), NB, axis=1)[:, None, :]
    turned = jnp.swapaxes(panels, 1, 2)

    cut = local_cols * 3 // 4
    chunks = [(0, 0, local_cols), (1, 0, local_cols), (2, 0, cut), (2, cut, local_cols)]

    order = row ^ jnp.arange(rows_n, dtype=jnp.int32)
    gathered = []
    for i, (j, lo, hi) in enumerate(chunks):
        token = gathered[i - 1] if i else mask
        shard = masked(turned, mask, token, j, lo, hi)
        if i == 0:
            inverse = prepared(ainv, order, shard, rows_n, part)
        gathered.append(lax.all_gather(shard, "pcol", axis=0, tiled=True))

    def columns(matrix, lo, hi):
        whole = matrix.shape[0]
        kept = matrix.reshape(whole, cols_n, local_cols)[:, :, lo:hi].reshape(whole, -1)
        return kept.T

    factors = []
    finished = []
    for (j, lo, hi), value in zip(chunks, gathered):
        pre = None
        if j == 1:
            pre = elimination([(columns(coupling[0], lo, hi), factors[0])])
        if j == 2:
            pre = elimination(
                [
                    (columns(coupling[1], lo, hi), factors[0]),
                    (columns(coupling[2], lo, hi), factors[1]),
                ]
            )
        factor, sent = products(value, inverse, 1, rows_n, pre)
        factors.append(factor)
        received = [exchange(sent[s - 1], "prow", rows_n, s) for s in range(1, rows_n)]
        _, (total,) = products(factor, inverse, 0, 1)
        for other in received:
            total = total + other
        count = hi - lo
        moved = lax.all_to_all((-total).reshape(cols_n, count, part), "pcol", 0, 0)
        moved = lax.all_to_all(moved.reshape(rows_n, ratio * count, part), "prow", 0, 0)
        moved = moved.reshape(rows_n, ratio, count, part).transpose(2, 1, 0, 3)
        finished.append(moved.reshape(count, local_rows))

    groups = [
        [(0, 0), (0, 1), (1, 1)],
        [(0, 2), (1, 2), (2, 2)],
        [(0, 3), (1, 3), (2, 3)],
        [(3, 2), (3, 3)],
    ]
    inner = {}
    for group in groups:
        terms = [inner_products(-finished[a], factors[b]) for a, b in group]
        flat = [t.reshape(-1, 128) for t in terms]
        joined = jnp.concatenate(flat, 0)
        summed = joined
        for s in range(1, rows_n):
            summed = summed + exchange(joined, "prow", rows_n, s)
        for (a, b), t, f in zip(group, terms, flat):
            inner[a, b] = summed[: f.shape[0]].reshape(t.shape)
            summed = summed[f.shape[0] :]

    def block(j, k):
        strips = []
        for a, (ja, lo, hi) in enumerate(chunks):
            if ja != j:
                continue
            pieces = [
                inner[a, b].reshape(hi - lo, cols_n, -1)
                for b, (kb, _, _) in enumerate(chunks)
                if kb == k
            ]
            strips.append(jnp.concatenate(pieces, 2).reshape(hi - lo, cols_n * local_cols))
        return jnp.concatenate(strips, 0)

    inner = [[block(j, k) for k in range(j, 3)] for j in range(3)]

    first, second, third = coupling[0], coupling[1], coupling[2]
    start = col * local_cols

    def own_rows(matrix):
        return lax.dynamic_slice_in_dim(matrix, start, local_cols, 0)

    def own_cols(matrix):
        return lax.dynamic_slice_in_dim(matrix, start, local_cols, 1)

    bridge = second - matmul(first, third)
    d0 = own_rows(dinv[0])
    d1 = own_rows(dinv[1])
    k0 = tdot(own_cols(first), dinv[0])
    k1 = tdot(own_cols(bridge), dinv[0])
    k2 = tdot(own_cols(third), dinv[1])
    diag_zero = d0 + inner[0][0]
    cross_one = inner[0][1] - matmul(d0, first)
    cross_two = inner[0][2] - matmul(d0, bridge)
    diag_one = inner[1][0] + (d1 + matmul(k0, first))
    cross_three = inner[1][1] + (matmul(k0, bridge) - matmul(d1, third))
    diag_two = inner[2][0] + (own_rows(dinv[2]) + matmul(k1, bridge) + matmul(k2, third))

    panel_parts = [[], [], []]
    for (j, lo, hi), value in zip(chunks, finished):
        panel_parts[j].append(value)
    xpanel = jnp.stack([jnp.concatenate(p, 0) for p in panel_parts], 0)
    xcross = jnp.stack([cross_one, cross_two, cross_three], 0)
    ydiag = jnp.stack([diag_zero, diag_one, diag_two], 0)
    return (jnp.swapaxes(xpanel, 1, 2), xcross, ydiag)


def solution(mesh):
    placed = (P("prow", "pcol"), P(None, "prow", "pcol"), P(), P(), P())
    return jax.shard_map(
        shards,
        mesh=mesh,
        in_specs=placed,
        out_specs=(P(None, "prow", "pcol"), P(None, "pcol", None), P(None, "pcol", None)),
        check_vma=False,
    )
```

time: 931 us -> 742 us (0.80)
  matrix products: 404 us -> 70.1 us
  Pallas kernels: 0 us -> 225 us
  waiting for transfers between devices: 267 us -> 195 us
  other arithmetic: 67.4 us -> 42.6 us
  local copies, waits for them, and re-layouts: 108 us -> 118 us
    dot_general x35 -> x25, matrix products: 386 us -> 49.8 us  [the longest x11 28.5 us: inner_products(): lax.dot_general(jnp.concatenate([high, low], 0), right[0], nt, preferred_...]
    pallas_call x0 -> x16, Pallas kernels: none -> 225 us  [the longest x8 166 us: products(): pl.pallas_call(functools.partial(product_kernel, first, count, tile_of(de...]
    all_gather x4, waiting for transfers between devices: 168 us -> 84.9 us  [shards(): gathered.append(lax.all_gather(shard, 'pcol', axis=0, tiled=True))]
    all_gather x3 -> x0, local copies, waits for them, and re-layouts: 39.9 us -> none  [shards(): lax.all_gather(shard[j, lo:hi], 'pcol', axis=0, tiled=True)]
    unnamed x112 -> x121, local copies, waits for them, and re-layouts: 11.1 us -> 49.4 us
    convert_element_type x6 -> x7, other arithmetic: 40.5 us -> 9.09 us  [split(): return (high.astype(jnp.bfloat16), (values - high).astype(jnp.bfloat16))]
    neg x2 -> x6, other arithmetic: 2.9 us -> 14.1 us  [the longest x4 11.4 us: shards(): moved = lax.all_to_all((-total).reshape(cols_n, count, part), 'pcol', 0, 0)]
    all_to_all x4, waiting for transfers between devices: 26.6 us -> 36.2 us  [shards(): moved = lax.all_to_all((-total).reshape(cols_n, count, part), 'pcol', 0, 0)]
  transfers between devices with their start and end apart: 36 -> 36, of which waited for: 12 -> 16; matrix products, arithmetic and copies ran while one was open for 30% -> 24% of each run, Pallas kernels for 0% -> 24%
where the time goes in v2:
time: 742 us; the launch traced here: 732 us
  Pallas kernels  225 us (30%)
  waiting for transfers between devices  195 us (26%)
  local copies, waits for them, and re-layouts  118 us (16%)
  matrix products  70.1 us (9%)
  starting transfers between devices  66 us (9%)
  other arithmetic  42.6 us (6%)
  between operations  14.8 us (2%)
    pallas_call x8, Pallas kernels, products(): pl.pallas_call(functools.partial(product_kernel, first, count, tile_of(de...  166 us
    all_gather x4, waiting for transfers between devices, shards(): gathered.append(lax.all_gather(shard, 'pcol', axis=0, tiled=True))  84.9 us
    ppermute x24, waiting for transfers between devices, exchange(): return lax.ppermute(value, axis, [(i, i ^ step) for i in range(size)])  69.4 us
    unnamed x121, local copies, waits for them, and re-layouts  49.4 us
    all_to_all x4, waiting for transfers between devices, shards(): moved = lax.all_to_all((-total).reshape(cols_n, count, part), 'pcol', 0, 0)  36.2 us
    pallas_call x3, Pallas kernels, elimination(): pl.pallas_call(functools.partial(elimination_kernel, len(pairs)), grid=(l...  35.5 us
    ppermute x24, starting transfers between devices, exchange(): return lax.ppermute(value, axis, [(i, i ^ step) for i in range(size)])  31 us
    dot_general x11, matrix products, inner_products(): lax.dot_general(jnp.concatenate([high, low], 0), right[0], nt, preferred_...  28.5 us
  transfers between devices with their start and end apart: 36, of which 16 were waited for; matrix products, arithmetic and copies ran while one was open for 24% of the time, Pallas kernels for 24%

profile of v2, /device:TPU:0, one launch (start us, length us, event | category | flops | bytes accessed | tf_op | source)
XLA Modules:
  0.0 731.5 jit_solution(7513356567893624280)
XLA Ops:
  11.1 84.9 %all-gather.5.cloned.1.call-done.refs_0_.token_ref = f32[512,4096]{1,0:T(8,128)} async-done(((f32[64,4096]{1,0:T(8,128)}), f32[512,4096]{1,0:T(8,128)}) %all-gather.5.cloned.1.call-update) | async-done | bytes 8388624 | tf_op jit(solution)/shard_map/all_gather | solution.py:277
  95.9 3.4 copy-done.9
  100.5 3.6 fusion.72
  104.0 2.5 copy.36
  106.6 2.7 copy.38
  110.5 23.0 %prepared.1 = (bf16[4,4096,512]{2,1,0:T(8,128)(2,1)S(1)}, bf16[4,4096,512]{2,1,0:T(8,128)(2,1)}) custom-call(s32[4]{0:T(128)S(1)} %iota_xor_fusion.order_ref, f32[4096,2048]{1,0:T(8,128)} %a_ref.1, f32[64,4096]{1,0:T(8,128)S(1)} %copy-done.6), custom_call_target="tpu_custom_call" | custom-call | flops 33554432 | bytes 67108864 | tf_op jit(solution)/shard_map/prepared/pallas_call | solution.py:95
  133.5 5.8 copy-done
  142.7 35.3 %products.8 = (bf16[512,4096]{1,0:T(8,128)(2,1)}, bf16[512,4096]{1,0:T(8,128)(2,1)}, f32[512,512]{1,0:T(8,128)}, f32[512,512]{1,0:T(8,128)}, f32[512,512]{1,0:T(8,128)}) custom-call(f32[512,4096]{1,0:T(8,128)} %all-gather.5.cloned.1.call-done.refs_0_.token_ref, bf16[4,4096,512]{2,1,0:T(8,128)(2,1)} %copy-done, ...), custom_call_target="tpu_custom_call" | custom-call | flops 19327352832 | bytes 41943040 | tf_op jit(solution)/shard_map/products/pallas_call | solution.py:190
  183.8 2.5 copy.37
  194.1 2.9 convolution_subtract_fusion
  196.9 3.4 copy-done.8
  201.3 13.7 %products.9 = f32[512,512]{1,0:T(8,128)} custom-call(bf16[512,4096]{1,0:T(8,128)(2,1)} %get-tuple-element.27.refs_0_.refs_2_, bf16[512,4096]{1,0:T(8,128)(2,1)} %get-tuple-element.28.refs_1_.refs_3_, bf16[4,4096,512]{2,1,0:T(8,128)(2,1)} %copy-done, bf16[4,4096,512]{2,1,0:T(8,128)(2,1)} %get-tuple-element.26.refs_2_.refs_3_), custom_call_target="tpu_custom_call" | custom-call | flops 6442450944 | bytes 25165824 | tf_op jit(solution)/shard_map/products/pallas_call | solution.py:190
  215.0 12.3 %collective-permute-done.1 = f32[512,512]{1,0:T(8,128)} collective-permute-done((f32[512,512]{1,0:T(8,128)}, f32[512,512]{1,0:T(8,128)}, u32[]{:S(2)}, u32[]{:S(2)}) %collective-permute-start.1) | collective-permute-done | bytes 1048608 | tf_op jit(solution)/shard_map/ppermute | solution.py:55
  227.3 3.7 add_negate_fusion.1
  231.0 4.5 all-to-all-start
  237.7 2.7 fusion.13
  242.2 2.6 convolution_add_fusion.5
  244.8 2.7 convolution_add_fusion.4
  250.0 35.1 %all-to-all-done = f32[8,64,512]{2,1,0:T(8,128)} async-done(((f32[8,64,512]{2,1,0:T(8,128)}), f32[8,64,512]{2,1,0:T(8,128)}, u32[]{:S(2)}, u32[]{:S(2)}) %all-to-all-start) | async-done | bytes 1048608 | tf_op jit(solution)/shard_map/all_to_all | solution.py:304
  285.1 4.2 all-to-all-start.1
  295.4 11.4 %elimination.3.refs_1_ = f32[512,4096]{1,0:T(8,128)} custom-call(bf16[512,512]{1,0:T(8,128)(2,1)S(1)} %copy-done.16, bf16[512,512]{1,0:T(8,128)(2,1)S(1)} %copy-done.15, bf16[512,4096]{1,0:T(8,128)(2,1)S(1)} %copy-done.3, bf16[512,4096]{1,0:T(8,128)(2,1)} %get-tuple-element.28.refs_1_.refs_3_), custom_call_target="tpu_custom_call" | custom-call | flops 6442450944 | bytes 16777216 | tf_op jit(solution)/shard_map/elimination/pallas_call | solution.py:228
  309.9 2.9 neg.42
  312.8 37.9 %products.10 = (bf16[512,4096]{1,0:T(8,128)(2,1)}, bf16[512,4096]{1,0:T(8,128)(2,1)}, f32[512,512]{1,0:T(8,128)}, f32[512,512]{1,0:T(8,128)}, f32[512,512]{1,0:T(8,128)}) custom-call(f32[512,4096]{1,0:T(8,128)} %all-gather.7.cloned.1.call-done.refs_0_.token_ref, f32[512,4096]{1,0:T(8,128)} %elimination.3.refs_1_, bf16[4,4096,512]{2,1,0:T(8,128)(2,1)} %copy-done, ...), custom_call_target="tpu_custom_call" | custom-call | flops 19327352832 | bytes 41943040 | tf_op jit(solution)/shard_map/products/pallas_call | solution.py:190
  355.3 2.9 copy.21
  358.2 13.7 %products.11 = f32[512,512]{1,0:T(8,128)} custom-call(bf16[512,4096]{1,0:T(8,128)(2,1)} %get-tuple-element.32.refs_0_.refs_6_, bf16[512,4096]{1,0:T(8,128)(2,1)} %get-tuple-element.33.refs_1_.refs_7_, bf16[4,4096,512]{2,1,0:T(8,128)(2,1)} %copy-done, bf16[4,4096,512]{2,1,0:T(8,128)(2,1)} %get-tuple-element.26.refs_2_.refs_3_), custom_call_target="tpu_custom_call" | custom-call | flops 6442450944 | bytes 25165824 | tf_op jit(solution)/shard_map/products/pallas_call | solution.py:190
  371.9 5.0 collective-permute-done.3
  376.9 23.1 %collective-permute-done.4 = f32[512,512]{1,0:T(8,128)S(1)} collective-permute-done((f32[512,512]{1,0:T(8,128)}, f32[512,512]{1,0:T(8,128)S(1)}, u32[]{:S(2)}, u32[]{:S(2)}) %collective-permute-start.4) | collective-permute-done | bytes 1048608 | tf_op jit(solution)/shard_map/ppermute | solution.py:55
  399.9 2.7 add_negate_fusion
  402.6 4.7 all-to-all-start.2
  407.3 4.2 fusion.62
  415.2 2.9 stack_reshape.6
  419.8 4.0 fusion.61
  430.9 9.7 %elimination.5.refs_1_ = f32[128,4096]{1,0:T(8,128)S(1)} custom-call(bf16[128,512]{1,0:T(8,128)(2,1)S(1)} %get-tuple-element.75.refs_0_, bf16[128,512]{1,0:T(8,128)(2,1)S(1)} %get-tuple-element.74.refs_1_, bf16[512,4096]{1,0:T(8,128)(2,1)} %get-tuple-element.27.refs_0_.refs_2_, bf16[512,4096]{1,0:T(8,128)(2,1)} %get-tuple-element.28.refs_1_.refs_3_, ...), custom_call_target="tpu_custom_call" | custom-call | flops 3221225472 | bytes 18874368 | tf_op jit(solution)/shard_map/elimination/pallas_call | solution.py:228
  441.9 4.2 all-to-all-start.3
  452.3 14.4 %elimination.4.refs_1_ = f32[384,4096]{1,0:T(8,128)} custom-call(bf16[384,512]{1,0:T(8,128)(2,1)S(1)} %copy-done.18, bf16[384,512]{1,0:T(8,128)(2,1)S(1)} %copy-done.17, bf16[512,4096]{1,0:T(8,128)(2,1)S(1)} %copy-done.4, bf16[512,4096]{1,0:T(8,128)(2,1)} %get-tuple-element.28.refs_1_.refs_3_, bf16[384,512]{1,0:T(8,128)(2,1)S(1)} %copy-done.19, ...), custom_call_target="tpu_custom_call" | custom-call | flops 9663676416 | bytes 23068672 | tf_op jit(solution)/shard_map/elimination/pallas_call | solution.py:228
  469.7 2.9 neg.44
  475.0 30.5 %products.12 = (bf16[384,4096]{1,0:T(8,128)(2,1)}, bf16[384,4096]{1,0:T(8,128)(2,1)}, f32[384,512]{1,0:T(8,128)}, f32[384,512]{1,0:T(8,128)}, f32[384,512]{1,0:T(8,128)}) custom-call(f32[384,4096]{1,0:T(8,128)} %all-gather.9.cloned.1.call-done.refs_0_.token_ref, f32[384,4096]{1,0:T(8,128)} %elimination.4.refs_1_, bf16[4,4096,512]{2,1,0:T(8,128)(2,1)} %copy-done, ...), custom_call_target="tpu_custom_call" | custom-call | flops 14495514624 | bytes 37748736 | tf_op jit(solution)/shard_map/products/pallas_call | solution.py:190
  507.5 2.6 fusion.28
  517.2 2.9 copy.23
  520.1 2.9 stack_reshape.7
  523.0 3.2 collective-permute-done.6
  526.2 2.9 collective-permute-start.14
  529.1 11.4 %products.13 = f32[384,512]{1,0:T(8,128)} custom-call(bf16[384,4096]{1,0:T(8,128)(2,1)} %get-tuple-element.37.refs_0_, bf16[384,4096]{1,0:T(8,128)(2,1)} %get-tuple-element.38.refs_1_, bf16[4,4096,512]{2,1,0:T(8,128)(2,1)} %copy-done, bf16[4,4096,512]{2,1,0:T(8,128)(2,1)} %get-tuple-element.26.refs_2_.refs_3_), custom_call_target="tpu_custom_call" | custom-call | flops 4831838208 | bytes 20971520 | tf_op jit(solution)/shard_map/products/pallas_call | solution.py:190
  540.6 7.2 collective-permute-done.7
  547.8 3.1 add_negate_fusion.2
  550.9 5.1 all-to-all-start.4
  556.0 7.5 %collective-permute-done.13 = f32[768,128]{1,0:T(8,128)} collective-permute-done((f32[768,128]{1,0:T(8,128)}, f32[768,128]{1,0:T(8,128)}, u32[]{:S(2)}, u32[]{:S(2)}) %collective-permute-start.13) | collective-permute-done | bytes 393248 | tf_op jit(solution)/shard_map/ppermute | solution.py:55
  567.9 2.8 copy-done.10
  571.5 3.4 fusion.27
  577.0 4.4 all-to-all-start.5
  581.4 4.0 fusion.60
  588.9 3.5 all-to-all-done.5
  592.4 2.5 copy.26
  594.9 2.6 reshape.126
  599.5 3.0 fusion.25
  616.9 4.6 collective-permute-done.16
  630.9 16.8 %products.14 = (bf16[128,4096]{1,0:T(8,128)(2,1)}, bf16[128,4096]{1,0:T(8,128)(2,1)}, f32[128,512]{1,0:T(8,128)}, f32[128,512]{1,0:T(8,128)}, f32[128,512]{1,0:T(8,128)}) custom-call(f32[128,4096]{1,0:T(8,128)} %all-gather.11.cloned.1.call-done.refs_0_, f32[128,4096]{1,0:T(8,128)} %copy-done.7, bf16[4,4096,512]{2,1,0:T(8,128)(2,1)} %copy-done, ...), custom_call_target="tpu_custom_call" | custom-call | flops 4831838208 | bytes 29360128 | tf_op jit(solution)/shard_map/products/pallas_call | solution.py:190
  659.2 6.6 products.15
  670.0 2.5 collective-permute-done.9
  674.4 4.0 all-to-all-start.6
  689.0 3.0 fusion
  692.0 2.7 fusion.2
  694.7 3.6 all-to-all-start.7
  706.4 3.0 fusion.33
  (267 shorter events, 166.5 us)
Async XLA Ops:
  7.2 88.8 %all-gather.5.cloned.1.call-start = ((), (), s32[]{:S(2)}) async-start(), calls=%async_computation.8 | async-start | bytes 9437184 | tf_op jit(solution)/shard_map/all_gather | solution.py:277
  9.9 86.0 %copy-start.2 = (f32[3,4096,64]{1,2,0:T(8,128)S(1)}, f32[3,4096,64]{1,2,0:T(8,128)}, u32[]{:S(2)}) copy-start(f32[3,4096,64]{1,2,0:T(8,128)} %param.6) | copy-start | bytes 9437188
  11.0 185.9 %all-gather.7.cloned.1.call-start = ((), (), s32[]{:S(2)}) async-start(), calls=%async_computation.9 | async-start | bytes 9437184 | tf_op jit(solution)/shard_map/all_gather | solution.py:277
  100.4 374.6 %all-gather.9.cloned.1.call-start = ((), (), s32[]{:S(2)}) async-start(), calls=%async_computation.10 | async-start | bytes 7077888 | tf_op jit(solution)/shard_map/all_gather | solution.py:277
  110.5 28.7 %copy-start.32 = (f32[3,512,512]{2,1,0:T(8,128)S(1)}, f32[3,512,512]{2,1,0:T(8,128)}, u32[]{:S(2)}) copy-start(f32[3,512,512]{2,1,0:T(8,128)} %param.9) | copy-start | bytes 9437188
  133.5 5.8 copy-start
  178.0 37.1 %collective-permute-start = (f32[512,512]{1,0:T(8,128)}, f32[512,512]{1,0:T(8,128)}, u32[]{:S(2)}, u32[]{:S(2)}) collective-permute-start(f32[512,512]{1,0:T(8,128)} %get-tuple-element.29), channel_id=1, source_target_pairs={{0,8},{8,0},{16,24},{24,16},{1,9},{9,1},{17,25},{25,17},{2,10},{10... | collective-permute-start | bytes 3145736 | tf_op jit(solution)/shard_map/ppermute | solution.py:55
  179.6 47.8 %collective-permute-start.1 = (f32[512,512]{1,0:T(8,128)}, f32[512,512]{1,0:T(8,128)}, u32[]{:S(2)}, u32[]{:S(2)}) collective-permute-start(f32[512,512]{1,0:T(8,128)} %get-tuple-element.30), channel_id=1, source_target_pairs={{0,16},{8,24},{16,0},{24,8},{1,17},{9,25},{17,1},{25,9},{2,18},{10... | collective-permute-start | bytes 3145736 | tf_op jit(solution)/shard_map/ppermute | solution.py:55
  181.0 46.3 %collective-permute-start.2 = (f32[512,512]{1,0:T(8,128)}, f32[512,512]{1,0:T(8,128)}, u32[]{:S(2)}, u32[]{:S(2)}) collective-permute-start(f32[512,512]{1,0:T(8,128)} %get-tuple-element.31), channel_id=1, source_target_pairs={{0,24},{8,16},{16,8},{24,0},{1,25},{9,17},{17,9},{25,1},{2,26},{10... | collective-permute-start | bytes 3145736 | tf_op jit(solution)/shard_map/ppermute | solution.py:55
  186.3 7.8 %copy-start.25 = (f32[3,512,512]{2,1,0:T(8,128)S(1)}, f32[3,512,512]{2,1,0:T(8,128)}, u32[]{:S(2)}) copy-start(f32[3,512,512]{2,1,0:T(8,128)} %param.8) | copy-start | bytes 9437188
  186.3 7.8 %copy-start.33 = (f32[1,512,512]{1,2,0:T(8,128)S(1)}, f32[1,512,512]{1,2,0:T(8,128)}, u32[]{:S(2)}) copy-start(f32[1,512,512]{1,2,0:T(8,128)} %copy.37) | copy-start | bytes 3145732
  231.0 54.1 %all-to-all-start = ((f32[8,64,512]{2,1,0:T(8,128)}), f32[8,64,512]{2,1,0:T(8,128)}, u32[]{:S(2)}, u32[]{:S(2)}) async-start(f32[8,64,512]{2,1,0:T(8,128)} %bitcast.166), calls=%async_computation | async-start | bytes 2097152 | tf_op jit(solution)/shard_map/all_to_all | solution.py:304
  235.5 5.0 copy-start.27
  235.5 12.0 %copy-start.37 = (f32[1,512,512]{1,2,0:T(8,128)S(1)}, f32[1,512,512]{1,2,0:T(8,128)}, u32[]{:S(2)}) copy-start(f32[1,512,512]{1,2,0:T(8,128)} %copy.36) | copy-start | bytes 3145732
  240.4 8.2 %copy-start.43 = (f32[512,8,48]{0,2,1:T(8,128)S(1)}, f32[512,8,48]{0,2,1:T(8,128)}, u32[]{:S(2)}) copy-start(f32[512,8,48]{0,2,1:T(8,128)} %slice.189) | copy-start | bytes 2359300
  240.4 8.2 %copy-start.44 = (f32[512,8,48]{0,2,1:T(8,128)S(1)}, f32[512,8,48]{0,2,1:T(8,128)}, u32[]{:S(2)}) copy-start(f32[512,8,48]{0,2,1:T(8,128)} %slice.190) | copy-start | bytes 2359300
  285.1 21.8 %all-to-all-start.1 = ((f32[4,128,512]{2,1,0:T(8,128)}), f32[4,128,512]{2,1,0:T(8,128)}, u32[]{:S(2)}, u32[]{:S(2)}) async-start(f32[4,128,512]{2,1,0:T(8,128)} %bitcast.3), calls=%async_computation.1 | async-start | bytes 2097152 | tf_op jit(solution)/shard_map/all_to_all | solution.py:305
  312.8 41.4 %copy-start.40 = (f32[64,4096]{1,0:T(8,128)S(1)}, f32[64,4096]{1,0:T(8,128)}, u32[]{:S(2)}) copy-start(f32[64,4096]{1,0:T(8,128)} %neg.42) | copy-start | bytes 3145732
  350.6 26.2 %collective-permute-start.3 = (f32[512,512]{1,0:T(8,128)}, f32[512,512]{1,0:T(8,128)S(1)}, u32[]{:S(2)}, u32[]{:S(2)}) collective-permute-start(f32[512,512]{1,0:T(8,128)} %get-tuple-element.34), channel_id=1, source_target_pairs={{0,8},{8,0},{16,24},{24,16},{1,9},{9,1},{17,25},{25,17},{2,10},{10... | collective-permute-start | bytes 3145736 | tf_op jit(solution)/shard_map/ppermute | solution.py:55
  352.6 47.3 %collective-permute-start.4 = (f32[512,512]{1,0:T(8,128)}, f32[512,512]{1,0:T(8,128)S(1)}, u32[]{:S(2)}, u32[]{:S(2)}) collective-permute-start(f32[512,512]{1,0:T(8,128)} %get-tuple-element.35), channel_id=1, source_target_pairs={{0,16},{8,24},{16,0},{24,8},{1,17},{9,25},{17,1},{25,9},{2,18},{10... | collective-permute-start | bytes 3145736 | tf_op jit(solution)/shard_map/ppermute | solution.py:55
  354.1 45.8 %collective-permute-start.5 = (f32[512,512]{1,0:T(8,128)}, f32[512,512]{1,0:T(8,128)S(1)}, u32[]{:S(2)}, u32[]{:S(2)}) collective-permute-start(f32[512,512]{1,0:T(8,128)} %get-tuple-element.36), channel_id=1, source_target_pairs={{0,24},{8,16},{16,8},{24,0},{1,25},{9,17},{17,9},{25,1},{2,26},{10... | collective-permute-start | bytes 3145736 | tf_op jit(solution)/shard_map/ppermute | solution.py:55
  402.6 39.3 %all-to-all-start.2 = ((f32[8,64,512]{2,1,0:T(8,128)}), f32[8,64,512]{2,1,0:T(8,128)}, u32[]{:S(2)}, u32[]{:S(2)}) async-start(f32[8,64,512]{2,1,0:T(8,128)} %bitcast.165), calls=%async_computation.2 | async-start | bytes 2097152 | tf_op jit(solution)/shard_map/all_to_all | solution.py:304
  407.3 4.2 copy-start.24
  407.3 4.2 copy-start.29
  418.1 5.8 copy-start.22
  418.1 5.8 copy-start.30
  441.9 24.8 %all-to-all-start.3 = ((f32[4,128,512]{2,1,0:T(8,128)}), f32[4,128,512]{2,1,0:T(8,128)}, u32[]{:S(2)}, u32[]{:S(2)}) async-start(f32[4,128,512]{2,1,0:T(8,128)} %bitcast.10), calls=%async_computation.3 | async-start | bytes 2097152 | tf_op jit(solution)/shard_map/all_to_all | solution.py:305
  475.0 32.6 %copy-start.28 = (bf16[512,4096]{1,0:T(8,128)(2,1)S(1)}, bf16[512,4096]{1,0:T(8,128)(2,1)}, u32[]{:S(2)}) copy-start(bf16[512,4096]{1,0:T(8,128)(2,1)} %get-tuple-element.32.refs_0_.refs_6_) | copy-start | bytes 12582916
  475.0 32.6 %copy-start.34 = (bf16[64,4096]{1,0:T(8,128)(2,1)S(1)}, bf16[64,4096]{1,0:T(8,128)(2,1)}, u32[]{:S(2)}) copy-start(bf16[64,4096]{1,0:T(8,128)(2,1)} %get-tuple-element.56) | copy-start | bytes 1572868
  505.5 6.5 copy-start.23
  505.5 20.7 %collective-permute-start.6 = (f32[384,512]{1,0:T(8,128)}, f32[384,512]{1,0:T(8,128)}, u32[]{:S(2)}, u32[]{:S(2)}) collective-permute-start(f32[384,512]{1,0:T(8,128)} %get-tuple-element.39), channel_id=1, source_target_pairs={{0,8},{8,0},{16,24},{24,16},{1,9},{9,1},{17,25},{25,17},{2,10},{10... | collective-permute-start | bytes 2359304 | tf_op jit(solution)/shard_map/ppermute | solution.py:55
  510.1 37.7 %collective-permute-start.7 = (f32[384,512]{1,0:T(8,128)}, f32[384,512]{1,0:T(8,128)}, u32[]{:S(2)}, u32[]{:S(2)}) collective-permute-start(f32[384,512]{1,0:T(8,128)} %get-tuple-element.40), channel_id=1, source_target_pairs={{0,16},{8,24},{16,0},{24,8},{1,17},{9,25},{17,1},{25,9},{2,18},{10... | collective-permute-start | bytes 2359304 | tf_op jit(solution)/shard_map/ppermute | solution.py:55
  511.7 36.1 %collective-permute-start.8 = (f32[384,512]{1,0:T(8,128)}, f32[384,512]{1,0:T(8,128)}, u32[]{:S(2)}, u32[]{:S(2)}) collective-permute-start(f32[384,512]{1,0:T(8,128)} %get-tuple-element.41), channel_id=1, source_target_pairs={{0,24},{8,16},{16,8},{24,0},{1,25},{9,17},{17,9},{25,1},{2,26},{10... | collective-permute-start | bytes 2359304 | tf_op jit(solution)/shard_map/ppermute | solution.py:55
  514.1 41.9 %collective-permute-start.12 = (f32[768,128]{1,0:T(8,128)}, f32[768,128]{1,0:T(8,128)}, u32[]{:S(2)}, u32[]{:S(2)}) collective-permute-start(f32[768,128]{1,0:T(8,128)} %constant_dynamic-update-slice_fusion), channel_id=1, source_target_pairs={{0,8},{8,0},{16,24},{24,16},{1,9},{9,1},{17,25},{25,17},{2,10},{10... | collective-permute-start | bytes 1179656 | tf_op jit(solution)/shard_map/ppermute | solution.py:55
  515.7 47.8 %collective-permute-start.13 = (f32[768,128]{1,0:T(8,128)}, f32[768,128]{1,0:T(8,128)}, u32[]{:S(2)}, u32[]{:S(2)}) collective-permute-start(f32[768,128]{1,0:T(8,128)} %constant_dynamic-update-slice_fusion), channel_id=1, source_target_pairs={{0,16},{8,24},{16,0},{24,8},{1,17},{9,25},{17,1},{25,9},{2,18},{10... | collective-permute-start | bytes 1179656 | tf_op jit(solution)/shard_map/ppermute | solution.py:55
  526.2 37.3 %collective-permute-start.14 = (f32[768,128]{1,0:T(8,128)}, f32[768,128]{1,0:T(8,128)}, u32[]{:S(2)}, u32[]{:S(2)}) collective-permute-start(f32[768,128]{1,0:T(8,128)} %constant_dynamic-update-slice_fusion), channel_id=1, source_target_pairs={{0,24},{8,16},{16,8},{24,0},{1,25},{9,17},{17,9},{25,1},{2,26},{10... | collective-permute-start | bytes 1179656 | tf_op jit(solution)/shard_map/ppermute | solution.py:55
  550.9 26.2 %all-to-all-start.4 = ((f32[8,48,512]{2,1,0:T(8,128)}), f32[8,48,512]{2,1,0:T(8,128)}, u32[]{:S(2)}, u32[]{:S(2)}) async-start(f32[8,48,512]{2,1,0:T(8,128)} %bitcast.167), calls=%async_computation.4 | async-start | bytes 1572864 | tf_op jit(solution)/shard_map/all_to_all | solution.py:304
  556.0 74.9 %all-gather.11.cloned.1.call-start = ((), (), s32[]{:S(2)}) async-start(), calls=%async_computation.11 | async-start | bytes 2359296 | tf_op jit(solution)/shard_map/all_gather | solution.py:277
  577.0 15.3 %all-to-all-start.5 = ((f32[4,96,512]{2,1,0:T(8,128)}), f32[4,96,512]{2,1,0:T(8,128)}, u32[]{:S(2)}, u32[]{:S(2)}) async-start(f32[4,96,512]{2,1,0:T(8,128)} %bitcast.22), calls=%async_computation.5 | async-start | bytes 1572864 | tf_op jit(solution)/shard_map/all_to_all | solution.py:305
  607.2 9.7 %collective-permute-start.15 = (f32[528,128]{1,0:T(8,128)}, f32[528,128]{1,0:T(8,128)}, u32[]{:S(2)}, u32[]{:S(2)}) collective-permute-start(f32[528,128]{1,0:T(8,128)} %constant_dynamic-update-slice_fusion.3), channel_id=1, source_target_pairs={{0,8},{8,0},{16,24},{24,16},{1,9},{9,1},{17,25},{25,17},{2,10},{10... | collective-permute-start | bytes 811016 | tf_op jit(solution)/shard_map/ppermute | solution.py:55
  608.6 12.9 %collective-permute-start.16 = (f32[528,128]{1,0:T(8,128)}, f32[528,128]{1,0:T(8,128)}, u32[]{:S(2)}, u32[]{:S(2)}) collective-permute-start(f32[528,128]{1,0:T(8,128)} %constant_dynamic-update-slice_fusion.3), channel_id=1, source_target_pairs={{0,16},{8,24},{16,0},{24,8},{1,17},{9,25},{17,1},{25,9},{2,18},{10... | collective-permute-start | bytes 811016 | tf_op jit(solution)/shard_map/ppermute | solution.py:55
  609.1 12.4 %collective-permute-start.17 = (f32[528,128]{1,0:T(8,128)}, f32[528,128]{1,0:T(8,128)}, u32[]{:S(2)}, u32[]{:S(2)}) collective-permute-start(f32[528,128]{1,0:T(8,128)} %constant_dynamic-update-slice_fusion.3), channel_id=1, source_target_pairs={{0,24},{8,16},{16,8},{24,0},{1,25},{9,17},{17,9},{25,1},{2,26},{10... | collective-permute-start | bytes 811016 | tf_op jit(solution)/shard_map/ppermute | solution.py:55
  630.9 16.8 %copy-start.31 = (bf16[64,4096]{1,0:T(8,128)(2,1)S(1)}, bf16[64,4096]{1,0:T(8,128)(2,1)}, u32[]{:S(2)}) copy-start(bf16[64,4096]{1,0:T(8,128)(2,1)} %get-tuple-element.54) | copy-start | bytes 1572868
  630.9 16.8 %copy-start.52 = (bf16[64,4096]{1,0:T(8,128)(2,1)S(1)}, bf16[64,4096]{1,0:T(8,128)(2,1)}, u32[]{:S(2)}) copy-start(bf16[64,4096]{1,0:T(8,128)(2,1)} %get-tuple-element.53) | copy-start | bytes 1572868
  630.9 18.6 %copy-start.36 = (bf16[64,4096]{1,0:T(8,128)(2,1)S(1)}, bf16[64,4096]{1,0:T(8,128)(2,1)}, u32[]{:S(2)}) copy-start(bf16[64,4096]{1,0:T(8,128)(2,1)} %get-tuple-element.56) | copy-start | bytes 1572868
  630.9 18.6 %copy-start.53 = (bf16[64,4096]{1,0:T(8,128)(2,1)S(1)}, bf16[64,4096]{1,0:T(8,128)(2,1)}, u32[]{:S(2)}) copy-start(bf16[64,4096]{1,0:T(8,128)(2,1)} %get-tuple-element.55) | copy-start | bytes 1572868
  647.7 3.6 copy-start.46
  647.7 4.0 copy-start.26
  653.2 12.6 %collective-permute-start.18 = (f32[176,128]{1,0:T(8,128)S(1)}, f32[176,128]{1,0:T(8,128)S(1)}, u32[]{:S(2)}, u32[]{:S(2)}) collective-permute-start(f32[176,128]{1,0:T(8,128)S(1)} %pad_maximum_fusion.16), channel_id=1, source_target_pairs={{0,8},{8,0},{16,24},{24,16},{1,9},{9,1},{17,25},{25,17},{2,10},{10... | collective-permute-start | bytes 270344 | tf_op jit(solution)/shard_map/ppermute | solution.py:55
  654.2 12.7 %collective-permute-start.19 = (f32[176,128]{1,0:T(8,128)S(1)}, f32[176,128]{1,0:T(8,128)S(1)}, u32[]{:S(2)}, u32[]{:S(2)}) collective-permute-start(f32[176,128]{1,0:T(8,128)S(1)} %pad_maximum_fusion.16), channel_id=1, source_target_pairs={{0,16},{8,24},{16,0},{24,8},{1,17},{9,25},{17,1},{25,9},{2,18},{10... | collective-permute-start | bytes 270344 | tf_op jit(solution)/shard_map/ppermute | solution.py:55
  655.4 11.5 %collective-permute-start.20 = (f32[176,128]{1,0:T(8,128)S(1)}, f32[176,128]{1,0:T(8,128)S(1)}, u32[]{:S(2)}, u32[]{:S(2)}) collective-permute-start(f32[176,128]{1,0:T(8,128)S(1)} %pad_maximum_fusion.16), channel_id=1, source_target_pairs={{0,24},{8,16},{16,8},{24,0},{1,25},{9,17},{17,9},{25,1},{2,26},{10... | collective-permute-start | bytes 270344 | tf_op jit(solution)/shard_map/ppermute | solution.py:55
  656.8 13.2 %collective-permute-start.10 = (f32[128,512]{1,0:T(8,128)}, f32[128,512]{1,0:T(8,128)}, u32[]{:S(2)}, u32[]{:S(2)}) collective-permute-start(f32[128,512]{1,0:T(8,128)} %get-tuple-element.45), channel_id=1, source_target_pairs={{0,16},{8,24},{16,0},{24,8},{1,17},{9,25},{17,1},{25,9},{2,18},{10... | collective-permute-start | bytes 786440 | tf_op jit(solution)/shard_map/ppermute | solution.py:55
  657.4 12.6 %collective-permute-start.11 = (f32[128,512]{1,0:T(8,128)}, f32[128,512]{1,0:T(8,128)}, u32[]{:S(2)}, u32[]{:S(2)}) collective-permute-start(f32[128,512]{1,0:T(8,128)} %get-tuple-element.46), channel_id=1, source_target_pairs={{0,24},{8,16},{16,8},{24,0},{1,25},{9,17},{17,9},{25,1},{2,26},{10... | collective-permute-start | bytes 786440 | tf_op jit(solution)/shard_map/ppermute | solution.py:55
  665.8 6.7 collective-permute-start.9
  668.4 23.6 %copy-start.49 = (f32[64,512]{1,0:T(8,128)S(1)}, f32[64,512]{1,0:T(8,128)}, u32[]{:S(2)}) copy-start(f32[64,512]{1,0:T(8,128)} %fusion.76) | copy-start | bytes 393220
  674.4 20.3 %all-to-all-start.6 = ((f32[8,16,512]{2,1,0:T(8,128)}), f32[8,16,512]{2,1,0:T(8,128)}, u32[]{:S(2)}, u32[]{:S(2)}) async-start(f32[8,16,512]{2,1,0:T(8,128)} %bitcast.168), calls=%async_computation.6 | async-start | bytes 524288 | tf_op jit(solution)/shard_map/all_to_all | solution.py:304
  694.7 9.6 %all-to-all-start.7 = ((f32[4,32,512]{2,1,0:T(8,128)}), f32[4,32,512]{2,1,0:T(8,128)S(1)}, u32[]{:S(2)}, u32[]{:S(2)}) async-start(f32[4,32,512]{2,1,0:T(8,128)} %bitcast.32), calls=%async_computation.7 | async-start | bytes 524288 | tf_op jit(solution)/shard_map/all_to_all | solution.py:305
  711.4 7.3 copy-start.41
  711.4 7.3 copy-start.42
  713.9 6.7 collective-permute-start.21
  715.4 5.2 collective-permute-start.22
  716.8 4.8 collective-permute-start.23
  718.7 5.2 copy-start.50
  718.7 5.2 copy-start.51
  (29 other events, 54.5 us)
Sparse Core Ops, SparseCore 0:
  11.1 84.7 all-gather.4
  100.5 80.5 all-gather.6
  201.4 86.0 all-gather.8
  571.6 29.4 all-gather.10
